TPU v7x, 32 devices: a whole 2x2x4 slice. The times are simulated.
32 devices in a mesh: dp: 16 (over z, y, core), fsdp: 2 (over x).
Axes of the slice: x: 2, y: 2, z: 4, core: 2. Of those that a mesh axis runs over, the one named last changes fastest.
Arguments:
- hidden: bfloat16 [16384, 1152], P(('dp', 'fsdp')), may hold values from -6 to 6
- text_ids: int32 [1024, 16], P(('dp', 'fsdp')), may hold values from 0 to 31999, as said below
- ln_gain: float32 [1152], replicated, may hold values from 0.5 to 1.5
- ln_bias: float32 [1152], replicated, may hold values from -2 to 2
- fc1_weight: bfloat16 [1152, 4304], P(None, 'fsdp'), may hold values from -0.1875 to 0.1875
- fc1_bias: float32 [4304], replicated, may hold values from -3 to 3
- fc2_weight: bfloat16 [4304, 1152], P('fsdp'), may hold values from -0.09375 to 0.09375
- fc2_bias: float32 [1152], replicated, may hold values from -3 to 3
- final_gain: float32 [1152], replicated, may hold values from 0.5 to 1.5
- final_bias: float32 [1152], replicated, may hold values from -0.2 to 0.2
- head_weight: bfloat16 [1152, 1152], replicated, may hold values from -0.1875 to 0.1875
- head_bias: float32 [1152], replicated, may hold values from -0.3 to 0.3
- image_emb: bfloat16 [1024, 1152], P(('dp', 'fsdp')), may hold values from -6 to 6
- teacher_logits: bfloat16 [1024, 12, 64], P('dp', None, 'fsdp'), may hold values from -12 to 12
- logit_scale: float32 [1], replicated, may hold values from 4 to 16
- logit_bias: float32 [1], replicated, may hold values from -3 to 0
Outputs:
- image_grad: float32 [1024, 1152], P(('dp', 'fsdp'))
Inputs may be any that keep to these rules, and one draw needn't show every extreme that they name: `text_ids`: 0 marks padding after a text's end; every text has at least one token and the tokens of a text come first.
All inputs are finite; a program needn't handle non-finite values.
Results may differ from a plain program's by a relative error of at most 0.0018.
Values may be sent and summed in bfloat16 or wider, within the bound.
A program may use at most 128 MiB of HBM per device.

v0:
```python
import jax
import jax.numpy as jnp
from jax import lax
from jax.sharding import PartitionSpec as P


def from_behind(array, axis, by):
    count = lax.axis_size(axis)
    return lax.ppermute(array, axis, [(i, (i + by) % count) for i in range(count)])


def layer_norm(values, gain, shift):
    centre = jnp.mean(values, axis=-1, keepdims=True)
    spread = jnp.mean((values - centre) ** 2, axis=-1, keepdims=True)
    return (values - centre) * lax.rsqrt(spread + 1e-06) * gain + shift


def on_device(
    hidden,
    text_ids,
    ln_gain,
    ln_bias,
    fc1_weight,
    fc1_bias,
    fc2_weight,
    fc2_bias,
    final_gain,
    final_bias,
    head_weight,
    head_bias,
    image_emb,
    teacher_logits,
    logit_scale,
    logit_bias,
):
    width = hidden.shape[1]
    texts_here, seq_len = text_ids.shape
    window = teacher_logits.shape[1]
    flat = hidden.astype(jnp.float32)
    normed = layer_norm(flat, ln_gain, ln_bias).astype(jnp.bfloat16)
    pre = (
        jnp.dot(
            normed,
            lax.all_gather(fc1_weight, "fsdp", axis=1, tiled=True),
            preferred_element_type=jnp.float32,
        )
        + fc1_bias
    )
    act = jax.nn.gelu(pre, approximate=True).astype(jnp.bfloat16)
    mixed = jnp.dot(
        act,
        lax.all_gather(fc2_weight, "fsdp", axis=0, tiled=True),
        preferred_element_type=jnp.float32,
    )
    out = flat + mixed + fc2_bias
    final = layer_norm(out, final_gain, final_bias).reshape(texts_here, seq_len, width)
    keep = (text_ids != 0).astype(jnp.float32)
    pooled = jnp.sum(final * keep[:, :, None], axis=1) / jnp.sum(keep, axis=1)[:, None]
    emb = (
        jnp.dot(pooled.astype(jnp.bfloat16), head_weight, preferred_element_type=jnp.float32)
        + head_bias
    )
    text_unit = (emb * lax.rsqrt(jnp.sum(emb * emb, axis=-1, keepdims=True) + 1e-06)).astype(
        jnp.bfloat16
    )
    group_units = lax.all_gather(text_unit, "fsdp", axis=0, tiled=True)
    images = image_emb.astype(jnp.float32)
    image_unit = (
        images * lax.rsqrt(jnp.sum(images * images, axis=-1, keepdims=True) + 1e-06)
    ).astype(jnp.bfloat16)
    scale = logit_scale[0]
    offset = logit_bias[0]

    def pair_term(units, pictures, tile):
        score = (
            scale
            * lax.dot_general(
                units, pictures, (((1,), (1,)), ((), ())), preferred_element_type=jnp.float32
            )
            + offset
        )
        weight = (jax.nn.sigmoid(score) - jax.nn.sigmoid(tile.astype(jnp.float32))).astype(
            jnp.bfloat16
        )
        return lax.dot_general(
            weight, units, (((0,), (0,)), ((), ())), preferred_element_type=jnp.float32
        )

    start_grad = jnp.zeros(image_unit.shape, jnp.float32)

    def turn_texts(step, carry):
        units, slab, total = carry
        tile = lax.dynamic_index_in_dim(slab, step, 1, keepdims=False)
        total = total + pair_term(units, image_unit, tile)
        units, slab = from_behind((units, slab), "dp", 1)
        return (units, slab, total)

    units, slab, total = lax.fori_loop(
        0, window - 1, turn_texts, (group_units, teacher_logits, start_grad)
    )
    total = total + pair_term(units, image_unit, slab[:, window - 1, :])
    return scale * total


def solution(mesh):
    placed = (
        P(("dp", "fsdp"), None),
        P(("dp", "fsdp"), None),
        P(),
        P(),
        P(None, "fsdp"),
        P(),
        P("fsdp", None),
        P(),
        P(),
        P(),
        P(),
        P(),
        P(("dp", "fsdp"), None),
        P("dp", None, "fsdp"),
        P(),
        P(),
    )
    return jax.shard_map(
        on_device, mesh=mesh, in_specs=placed, out_specs=P(("dp", "fsdp"), None), check_vma=False
    )
```

profile of v0, /device:TPU:0, one launch (start us, length us, event | category | flops | bytes accessed | tf_op | source)
XLA Modules:
  0.0 392.1 jit_solution(11806749970793733421)
XLA Ops:
  6.5 0.7 all-gather.3.cloned.1.call-update
  7.3 0.0 all-gather.5.cloned.1.call-start
  7.3 0.7 all-gather.5.cloned.1.call-update
  8.1 0.1 copy.17
  9.5 0.1 fusion.53
  9.6 1.5 convert_reduce_fusion
  11.1 1.7 fusion.31
  12.9 0.1 fusion.54
  13.0 121.9 %all-gather.3.cloned.1.call-done = bf16[1152,4304]{0,1:T(8,128)(2,1)} async-done(((bf16[1152,2152]{0,1:T(8,128)(2,1)}), bf16[1152,4304]{0,1:T(8,128)(2,1)}) %all-gather.3.cloned.1.call-update) | async-done | bytes 9916432 | tf_op jit(solution)/shard_map/all_gather | solution.py:44
  134.9 124.9 %all-gather.5.cloned.1.call-done = bf16[4304,1152]{1,0:T(8,128)(2,1)} async-done(((bf16[2152,1152]{1,0:T(8,128)(2,1)}), bf16[4304,1152]{1,0:T(8,128)(2,1)}) %all-gather.5.cloned.1.call-update) | async-done | bytes 9916432 | tf_op jit(solution)/shard_map/all_gather | solution.py:52
  259.8 0.0 copy-start.6
  259.8 23.0 %fusion.73 = (f32[512]{0:T(512)S(1)}, f32[512,1152]{1,0:T(8,128)}) fusion(f32[1152]{0:T(1024)S(1)} %copy-done.9, bf16[4304,1152]{1,0:T(8,128)(2,1)} %all-gather.5.cloned.1.call-done, bf16[1152,4304]{0,1:T(8,128)(2,1)} %all-gather.3.cloned.1.call-done, f32[4304]{0:T(1024)S(1)} %copy-done.8, bf16[512,1152]{1,0:T(8,128)(2,1)} %param.18, ...), kind=kOutput, calls=%fused_computation.91 | convolution fusion | flops 10182344704 | bytes 23408960 | tf_op jit(solution)/shard_map/dot_general | solution.py:50
  282.9 2.2 multiply_reduce_fusion.1
  285.1 0.1 copy-done.1
  285.2 0.9 multiply_reduce_fusion
  286.1 0.7 multiply_reduce_fusion.2
  286.8 0.1 multiply_convert_fusion
  286.9 5.0 %all_gather.11 = bf16[64,1152]{1,0:T(8,128)(2,1)S(1)} all-gather(bf16[32,1152]{1,0:T(8,128)(2,1)S(1)} %multiply_convert_fusion), channel_id=1, replica_groups=mesh['dp'=16,'fsdp'=2] {'fsdp'}, dimensions={0}, use_global_device_ids=true | all-gather | bytes 221184 | tf_op jit(solution)/shard_map/all_gather | solution.py:66
  292.0 92.3 %while.18 = (s32[]{:T(128)}, bf16[64,1152]{1,0:T(8,128)(2,1)S(1)}, bf16[64,12,32]{0,2,1:T(8,128)(2,1)S(1)}, f32[32,1152]{1,0:T(8,128)S(1)}, f32[]{:T(128)}, /*in...) while((s32[]{:T(128)}, bf16[64,1152]{1,0:T(8,128)(2,1)S(1)}, ...), condition=%wide.region_9.10_spmd.clone, body=%wide.region_8.9_spmd.clone.sunk | while | flops 9533443 | bytes 1851587 | solution.py:98
  292.0 0.1 collective-permute-start
  292.1 1.6 collective-permute-start.1
  293.7 1.7 convolution_add_fusion.4
  295.4 5.0 %collective-permute-done.1 = bf16[64,12,32]{0,2,1:T(8,128)(2,1)S(1)} collective-permute-done((bf16[64,12,32]{0,2,1:T(8,128)(2,1)S(1)}, bf16[64,12,32]{0,2,1:T(8,128)(2,1)S(1)}, u32[]{:S(2)}, u32[]{:S(2)}) %collective-permute-start.1) | collective-permute-done | bytes 49184 | tf_op jit(solution)/shard_map/while/body/eval_jaxpr/ppermute | solution.py:9
  300.4 0.1 collective-permute-start
  300.5 0.1 collective-permute-start.1
  300.5 1.7 convolution_add_fusion.4
  302.2 6.5 %collective-permute-done.1 = bf16[64,12,32]{0,2,1:T(8,128)(2,1)S(1)} collective-permute-done((bf16[64,12,32]{0,2,1:T(8,128)(2,1)S(1)}, bf16[64,12,32]{0,2,1:T(8,128)(2,1)S(1)}, u32[]{:S(2)}, u32[]{:S(2)}) %collective-permute-start.1) | collective-permute-done | bytes 49184 | tf_op jit(solution)/shard_map/while/body/eval_jaxpr/ppermute | solution.py:9
  308.8 0.1 collective-permute-start
  308.9 0.1 collective-permute-start.1
  308.9 1.7 convolution_add_fusion.4
  310.6 6.5 %collective-permute-done.1 = bf16[64,12,32]{0,2,1:T(8,128)(2,1)S(1)} collective-permute-done((bf16[64,12,32]{0,2,1:T(8,128)(2,1)S(1)}, bf16[64,12,32]{0,2,1:T(8,128)(2,1)S(1)}, u32[]{:S(2)}, u32[]{:S(2)}) %collective-permute-start.1) | collective-permute-done | bytes 49184 | tf_op jit(solution)/shard_map/while/body/eval_jaxpr/ppermute | solution.py:9
  317.2 0.1 collective-permute-start
  317.3 0.1 collective-permute-start.1
  317.3 1.7 convolution_add_fusion.4
  319.0 6.5 %collective-permute-done.1 = bf16[64,12,32]{0,2,1:T(8,128)(2,1)S(1)} collective-permute-done((bf16[64,12,32]{0,2,1:T(8,128)(2,1)S(1)}, bf16[64,12,32]{0,2,1:T(8,128)(2,1)S(1)}, u32[]{:S(2)}, u32[]{:S(2)}) %collective-permute-start.1) | collective-permute-done | bytes 49184 | tf_op jit(solution)/shard_map/while/body/eval_jaxpr/ppermute | solution.py:9
  325.6 0.1 collective-permute-start
  325.6 0.1 collective-permute-start.1
  325.7 1.7 convolution_add_fusion.4
  327.4 6.5 %collective-permute-done.1 = bf16[64,12,32]{0,2,1:T(8,128)(2,1)S(1)} collective-permute-done((bf16[64,12,32]{0,2,1:T(8,128)(2,1)S(1)}, bf16[64,12,32]{0,2,1:T(8,128)(2,1)S(1)}, u32[]{:S(2)}, u32[]{:S(2)}) %collective-permute-start.1) | collective-permute-done | bytes 49184 | tf_op jit(solution)/shard_map/while/body/eval_jaxpr/ppermute | solution.py:9
  334.0 0.1 collective-permute-start
  334.0 0.1 collective-permute-start.1
  334.1 1.7 convolution_add_fusion.4
  335.8 6.5 %collective-permute-done.1 = bf16[64,12,32]{0,2,1:T(8,128)(2,1)S(1)} collective-permute-done((bf16[64,12,32]{0,2,1:T(8,128)(2,1)S(1)}, bf16[64,12,32]{0,2,1:T(8,128)(2,1)S(1)}, u32[]{:S(2)}, u32[]{:S(2)}) %collective-permute-start.1) | collective-permute-done | bytes 49184 | tf_op jit(solution)/shard_map/while/body/eval_jaxpr/ppermute | solution.py:9
  342.3 0.1 collective-permute-start
  342.4 0.1 collective-permute-start.1
  342.5 1.7 convolution_add_fusion.4
  344.2 6.5 %collective-permute-done.1 = bf16[64,12,32]{0,2,1:T(8,128)(2,1)S(1)} collective-permute-done((bf16[64,12,32]{0,2,1:T(8,128)(2,1)S(1)}, bf16[64,12,32]{0,2,1:T(8,128)(2,1)S(1)}, u32[]{:S(2)}, u32[]{:S(2)}) %collective-permute-start.1) | collective-permute-done | bytes 49184 | tf_op jit(solution)/shard_map/while/body/eval_jaxpr/ppermute | solution.py:9
  350.7 0.1 collective-permute-start
  350.8 0.1 collective-permute-start.1
  350.9 1.7 convolution_add_fusion.4
  352.6 6.5 %collective-permute-done.1 = bf16[64,12,32]{0,2,1:T(8,128)(2,1)S(1)} collective-permute-done((bf16[64,12,32]{0,2,1:T(8,128)(2,1)S(1)}, bf16[64,12,32]{0,2,1:T(8,128)(2,1)S(1)}, u32[]{:S(2)}, u32[]{:S(2)}) %collective-permute-start.1) | collective-permute-done | bytes 49184 | tf_op jit(solution)/shard_map/while/body/eval_jaxpr/ppermute | solution.py:9
  359.1 0.1 collective-permute-start
  359.2 0.1 collective-permute-start.1
  359.3 1.7 convolution_add_fusion.4
  361.0 6.5 %collective-permute-done.1 = bf16[64,12,32]{0,2,1:T(8,128)(2,1)S(1)} collective-permute-done((bf16[64,12,32]{0,2,1:T(8,128)(2,1)S(1)}, bf16[64,12,32]{0,2,1:T(8,128)(2,1)S(1)}, u32[]{:S(2)}, u32[]{:S(2)}) %collective-permute-start.1) | collective-permute-done | bytes 49184 | tf_op jit(solution)/shard_map/while/body/eval_jaxpr/ppermute | solution.py:9
  367.5 0.1 collective-permute-start
  367.6 0.1 collective-permute-start.1
  367.7 1.7 convolution_add_fusion.4
  369.4 6.5 %collective-permute-done.1 = bf16[64,12,32]{0,2,1:T(8,128)(2,1)S(1)} collective-permute-done((bf16[64,12,32]{0,2,1:T(8,128)(2,1)S(1)}, bf16[64,12,32]{0,2,1:T(8,128)(2,1)S(1)}, u32[]{:S(2)}, u32[]{:S(2)}) %collective-permute-start.1) | collective-permute-done | bytes 49184 | tf_op jit(solution)/shard_map/while/body/eval_jaxpr/ppermute | solution.py:9
  375.9 0.1 collective-permute-start
  376.0 0.1 collective-permute-start.1
  376.1 1.7 convolution_add_fusion.4
  377.7 6.5 %collective-permute-done.1 = bf16[64,12,32]{0,2,1:T(8,128)(2,1)S(1)} collective-permute-done((bf16[64,12,32]{0,2,1:T(8,128)(2,1)S(1)}, bf16[64,12,32]{0,2,1:T(8,128)(2,1)S(1)}, u32[]{:S(2)}, u32[]{:S(2)}) %collective-permute-start.1) | collective-permute-done | bytes 49184 | tf_op jit(solution)/shard_map/while/body/eval_jaxpr/ppermute | solution.py:9
  384.3 1.0 fusion.35
  (65 shorter events, 0.4 us)
Async XLA Ops:
  6.5 279.6 %copy-start = (bf16[1152,1152]{1,0:T(8,128)(2,1)S(1)}, bf16[1152,1152]{1,0:T(8,128)(2,1)}, u32[]{:S(2)}) copy-start(bf16[1152,1152]{1,0:T(8,128)(2,1)} %param.28) | copy-start | bytes 7962628
  6.5 128.4 %all-gather.3.cloned.1.call-start = ((), (), s32[]{:S(2)}) async-start(), calls=%async_computation | async-start | bytes 14874624 | tf_op jit(solution)/shard_map/all_gather | solution.py:44
  7.3 0.8 copy-start.4
  7.3 2.2 copy-start.3
  7.3 252.5 %all-gather.5.cloned.1.call-start = ((), (), s32[]{:S(2)}) async-start(), calls=%async_computation.1 | async-start | bytes 14874624 | tf_op jit(solution)/shard_map/all_gather | solution.py:52
  8.0 251.7 %copy-start.8 = (f32[4304]{0:T(1024)S(1)}, f32[4304]{0:T(1024)}, u32[]{:S(2)}) copy-start(f32[4304]{0:T(1024)} %param.23) | copy-start | bytes 51652
  8.0 251.7 %copy-start.9 = (f32[1152]{0:T(1024)S(1)}, f32[1152]{0:T(1024)}, u32[]{:S(2)}) copy-start(f32[1152]{0:T(1024)} %param.25) | copy-start | bytes 13828
  8.0 251.7 %copy-start.10 = (f32[1152]{0:T(1024)S(1)}, f32[1152]{0:T(1024)}, u32[]{:S(2)}) copy-start(f32[1152]{0:T(1024)} %param.21) | copy-start | bytes 13828
  8.1 251.7 %copy-start.11 = (f32[1152]{0:T(1024)S(1)}, f32[1152]{0:T(1024)}, u32[]{:S(2)}) copy-start(f32[1152]{0:T(1024)} %param.20) | copy-start | bytes 13828
  259.8 25.3 %copy-start.6 = (f32[1152]{0:T(1024)S(1)}, f32[1152]{0:T(1024)}, u32[]{:S(2)}) copy-start(f32[1152]{0:T(1024)} %param.26) | copy-start | bytes 13828
  282.8 2.4 copy-start.1
  282.8 2.4 copy-start.5
  282.8 3.3 copy-start.7
  285.2 6.8 %copy-start.2 = (bf16[64,12,32]{0,2,1:T(8,128)(2,1)S(1)}, bf16[64,12,32]{0,2,1:T(8,128)(2,1)}, u32[]{:S(2)}) copy-start(bf16[64,12,32]{0,2,1:T(8,128)(2,1)} %param.31) | copy-start | bytes 147460
  292.0 8.4 %collective-permute-start = (bf16[64,1152]{1,0:T(8,128)(2,1)S(1)}, bf16[64,1152]{1,0:T(8,128)(2,1)S(1)}, u32[]{:S(2)}, u32[]{:S(2)}) collective-permute-start(bf16[64,1152]{1,0:T(8,128)(2,1)S(1)} %copy.23), channel_id=1, source_target_pairs={{0,2},{2,4},{4,6},{6,8},{8,10},{10,12},{12,14},{14,16},{16,18},{18... | collective-permute-start | bytes 442376 | tf_op jit(solution)/shard_map/while/body/eval_jaxpr/ppermute | solution.py:9
  292.1 8.3 %collective-permute-start.1 = (bf16[64,12,32]{0,2,1:T(8,128)(2,1)S(1)}, bf16[64,12,32]{0,2,1:T(8,128)(2,1)S(1)}, u32[]{:S(2)}, u32[]{:S(2)}) collective-permute-start(bf16[64,12,32]{0,2,1:T(8,128)(2,1)S(1)} %copy.24), channel_id=1, source_target_pairs={{0,2},{2,4},{4,6},{6,8},{8,10},{10,12},{12,14},{14,16},{16,18},{18... | collective-permute-start | bytes 147464 | tf_op jit(solution)/shard_map/while/body/eval_jaxpr/ppermute | solution.py:9
  300.4 8.4 %collective-permute-start = (bf16[64,1152]{1,0:T(8,128)(2,1)S(1)}, bf16[64,1152]{1,0:T(8,128)(2,1)S(1)}, u32[]{:S(2)}, u32[]{:S(2)}) collective-permute-start(bf16[64,1152]{1,0:T(8,128)(2,1)S(1)} %copy.23), channel_id=1, source_target_pairs={{0,2},{2,4},{4,6},{6,8},{8,10},{10,12},{12,14},{14,16},{16,18},{18... | collective-permute-start | bytes 442376 | tf_op jit(solution)/shard_map/while/body/eval_jaxpr/ppermute | solution.py:9
  300.5 8.3 %collective-permute-start.1 = (bf16[64,12,32]{0,2,1:T(8,128)(2,1)S(1)}, bf16[64,12,32]{0,2,1:T(8,128)(2,1)S(1)}, u32[]{:S(2)}, u32[]{:S(2)}) collective-permute-start(bf16[64,12,32]{0,2,1:T(8,128)(2,1)S(1)} %copy.24), channel_id=1, source_target_pairs={{0,2},{2,4},{4,6},{6,8},{8,10},{10,12},{12,14},{14,16},{16,18},{18... | collective-permute-start | bytes 147464 | tf_op jit(solution)/shard_map/while/body/eval_jaxpr/ppermute | solution.py:9
  308.8 8.4 %collective-permute-start = (bf16[64,1152]{1,0:T(8,128)(2,1)S(1)}, bf16[64,1152]{1,0:T(8,128)(2,1)S(1)}, u32[]{:S(2)}, u32[]{:S(2)}) collective-permute-start(bf16[64,1152]{1,0:T(8,128)(2,1)S(1)} %copy.23), channel_id=1, source_target_pairs={{0,2},{2,4},{4,6},{6,8},{8,10},{10,12},{12,14},{14,16},{16,18},{18... | collective-permute-start | bytes 442376 | tf_op jit(solution)/shard_map/while/body/eval_jaxpr/ppermute | solution.py:9
  308.9 8.3 %collective-permute-start.1 = (bf16[64,12,32]{0,2,1:T(8,128)(2,1)S(1)}, bf16[64,12,32]{0,2,1:T(8,128)(2,1)S(1)}, u32[]{:S(2)}, u32[]{:S(2)}) collective-permute-start(bf16[64,12,32]{0,2,1:T(8,128)(2,1)S(1)} %copy.24), channel_id=1, source_target_pairs={{0,2},{2,4},{4,6},{6,8},{8,10},{10,12},{12,14},{14,16},{16,18},{18... | collective-permute-start | bytes 147464 | tf_op jit(solution)/shard_map/while/body/eval_jaxpr/ppermute | solution.py:9
  317.2 8.4 %collective-permute-start = (bf16[64,1152]{1,0:T(8,128)(2,1)S(1)}, bf16[64,1152]{1,0:T(8,128)(2,1)S(1)}, u32[]{:S(2)}, u32[]{:S(2)}) collective-permute-start(bf16[64,1152]{1,0:T(8,128)(2,1)S(1)} %copy.23), channel_id=1, source_target_pairs={{0,2},{2,4},{4,6},{6,8},{8,10},{10,12},{12,14},{14,16},{16,18},{18... | collective-permute-start | bytes 442376 | tf_op jit(solution)/shard_map/while/body/eval_jaxpr/ppermute | solution.py:9
  317.3 8.3 %collective-permute-start.1 = (bf16[64,12,32]{0,2,1:T(8,128)(2,1)S(1)}, bf16[64,12,32]{0,2,1:T(8,128)(2,1)S(1)}, u32[]{:S(2)}, u32[]{:S(2)}) collective-permute-start(bf16[64,12,32]{0,2,1:T(8,128)(2,1)S(1)} %copy.24), channel_id=1, source_target_pairs={{0,2},{2,4},{4,6},{6,8},{8,10},{10,12},{12,14},{14,16},{16,18},{18... | collective-permute-start | bytes 147464 | tf_op jit(solution)/shard_map/while/body/eval_jaxpr/ppermute | solution.py:9
  325.6 8.4 %collective-permute-start = (bf16[64,1152]{1,0:T(8,128)(2,1)S(1)}, bf16[64,1152]{1,0:T(8,128)(2,1)S(1)}, u32[]{:S(2)}, u32[]{:S(2)}) collective-permute-start(bf16[64,1152]{1,0:T(8,128)(2,1)S(1)} %copy.23), channel_id=1, source_target_pairs={{0,2},{2,4},{4,6},{6,8},{8,10},{10,12},{12,14},{14,16},{16,18},{18... | collective-permute-start | bytes 442376 | tf_op jit(solution)/shard_map/while/body/eval_jaxpr/ppermute | solution.py:9
  325.6 8.3 %collective-permute-start.1 = (bf16[64,12,32]{0,2,1:T(8,128)(2,1)S(1)}, bf16[64,12,32]{0,2,1:T(8,128)(2,1)S(1)}, u32[]{:S(2)}, u32[]{:S(2)}) collective-permute-start(bf16[64,12,32]{0,2,1:T(8,128)(2,1)S(1)} %copy.24), channel_id=1, source_target_pairs={{0,2},{2,4},{4,6},{6,8},{8,10},{10,12},{12,14},{14,16},{16,18},{18... | collective-permute-start | bytes 147464 | tf_op jit(solution)/shard_map/while/body/eval_jaxpr/ppermute | solution.py:9
  334.0 8.4 %collective-permute-start = (bf16[64,1152]{1,0:T(8,128)(2,1)S(1)}, bf16[64,1152]{1,0:T(8,128)(2,1)S(1)}, u32[]{:S(2)}, u32[]{:S(2)}) collective-permute-start(bf16[64,1152]{1,0:T(8,128)(2,1)S(1)} %copy.23), channel_id=1, source_target_pairs={{0,2},{2,4},{4,6},{6,8},{8,10},{10,12},{12,14},{14,16},{16,18},{18... | collective-permute-start | bytes 442376 | tf_op jit(solution)/shard_map/while/body/eval_jaxpr/ppermute | solution.py:9
  334.0 8.3 %collective-permute-start.1 = (bf16[64,12,32]{0,2,1:T(8,128)(2,1)S(1)}, bf16[64,12,32]{0,2,1:T(8,128)(2,1)S(1)}, u32[]{:S(2)}, u32[]{:S(2)}) collective-permute-start(bf16[64,12,32]{0,2,1:T(8,128)(2,1)S(1)} %copy.24), channel_id=1, source_target_pairs={{0,2},{2,4},{4,6},{6,8},{8,10},{10,12},{12,14},{14,16},{16,18},{18... | collective-permute-start | bytes 147464 | tf_op jit(solution)/shard_map/while/body/eval_jaxpr/ppermute | solution.py:9
  342.3 8.4 %collective-permute-start = (bf16[64,1152]{1,0:T(8,128)(2,1)S(1)}, bf16[64,1152]{1,0:T(8,128)(2,1)S(1)}, u32[]{:S(2)}, u32[]{:S(2)}) collective-permute-start(bf16[64,1152]{1,0:T(8,128)(2,1)S(1)} %copy.23), channel_id=1, source_target_pairs={{0,2},{2,4},{4,6},{6,8},{8,10},{10,12},{12,14},{14,16},{16,18},{18... | collective-permute-start | bytes 442376 | tf_op jit(solution)/shard_map/while/body/eval_jaxpr/ppermute | solution.py:9
  342.4 8.3 %collective-permute-start.1 = (bf16[64,12,32]{0,2,1:T(8,128)(2,1)S(1)}, bf16[64,12,32]{0,2,1:T(8,128)(2,1)S(1)}, u32[]{:S(2)}, u32[]{:S(2)}) collective-permute-start(bf16[64,12,32]{0,2,1:T(8,128)(2,1)S(1)} %copy.24), channel_id=1, source_target_pairs={{0,2},{2,4},{4,6},{6,8},{8,10},{10,12},{12,14},{14,16},{16,18},{18... | collective-permute-start | bytes 147464 | tf_op jit(solution)/shard_map/while/body/eval_jaxpr/ppermute | solution.py:9
  350.7 8.4 %collective-permute-start = (bf16[64,1152]{1,0:T(8,128)(2,1)S(1)}, bf16[64,1152]{1,0:T(8,128)(2,1)S(1)}, u32[]{:S(2)}, u32[]{:S(2)}) collective-permute-start(bf16[64,1152]{1,0:T(8,128)(2,1)S(1)} %copy.23), channel_id=1, source_target_pairs={{0,2},{2,4},{4,6},{6,8},{8,10},{10,12},{12,14},{14,16},{16,18},{18... | collective-permute-start | bytes 442376 | tf_op jit(solution)/shard_map/while/body/eval_jaxpr/ppermute | solution.py:9
  350.8 8.3 %collective-permute-start.1 = (bf16[64,12,32]{0,2,1:T(8,128)(2,1)S(1)}, bf16[64,12,32]{0,2,1:T(8,128)(2,1)S(1)}, u32[]{:S(2)}, u32[]{:S(2)}) collective-permute-start(bf16[64,12,32]{0,2,1:T(8,128)(2,1)S(1)} %copy.24), channel_id=1, source_target_pairs={{0,2},{2,4},{4,6},{6,8},{8,10},{10,12},{12,14},{14,16},{16,18},{18... | collective-permute-start | bytes 147464 | tf_op jit(solution)/shard_map/while/body/eval_jaxpr/ppermute | solution.py:9
  359.1 8.4 %collective-permute-start = (bf16[64,1152]{1,0:T(8,128)(2,1)S(1)}, bf16[64,1152]{1,0:T(8,128)(2,1)S(1)}, u32[]{:S(2)}, u32[]{:S(2)}) collective-permute-start(bf16[64,1152]{1,0:T(8,128)(2,1)S(1)} %copy.23), channel_id=1, source_target_pairs={{0,2},{2,4},{4,6},{6,8},{8,10},{10,12},{12,14},{14,16},{16,18},{18... | collective-permute-start | bytes 442376 | tf_op jit(solution)/shard_map/while/body/eval_jaxpr/ppermute | solution.py:9
  359.2 8.3 %collective-permute-start.1 = (bf16[64,12,32]{0,2,1:T(8,128)(2,1)S(1)}, bf16[64,12,32]{0,2,1:T(8,128)(2,1)S(1)}, u32[]{:S(2)}, u32[]{:S(2)}) collective-permute-start(bf16[64,12,32]{0,2,1:T(8,128)(2,1)S(1)} %copy.24), channel_id=1, source_target_pairs={{0,2},{2,4},{4,6},{6,8},{8,10},{10,12},{12,14},{14,16},{16,18},{18... | collective-permute-start | bytes 147464 | tf_op jit(solution)/shard_map/while/body/eval_jaxpr/ppermute | solution.py:9
  367.5 8.4 %collective-permute-start = (bf16[64,1152]{1,0:T(8,128)(2,1)S(1)}, bf16[64,1152]{1,0:T(8,128)(2,1)S(1)}, u32[]{:S(2)}, u32[]{:S(2)}) collective-permute-start(bf16[64,1152]{1,0:T(8,128)(2,1)S(1)} %copy.23), channel_id=1, source_target_pairs={{0,2},{2,4},{4,6},{6,8},{8,10},{10,12},{12,14},{14,16},{16,18},{18... | collective-permute-start | bytes 442376 | tf_op jit(solution)/shard_map/while/body/eval_jaxpr/ppermute | solution.py:9
  367.6 8.3 %collective-permute-start.1 = (bf16[64,12,32]{0,2,1:T(8,128)(2,1)S(1)}, bf16[64,12,32]{0,2,1:T(8,128)(2,1)S(1)}, u32[]{:S(2)}, u32[]{:S(2)}) collective-permute-start(bf16[64,12,32]{0,2,1:T(8,128)(2,1)S(1)} %copy.24), channel_id=1, source_target_pairs={{0,2},{2,4},{4,6},{6,8},{8,10},{10,12},{12,14},{14,16},{16,18},{18... | collective-permute-start | bytes 147464 | tf_op jit(solution)/shard_map/while/body/eval_jaxpr/ppermute | solution.py:9
  375.9 8.4 %collective-permute-start = (bf16[64,1152]{1,0:T(8,128)(2,1)S(1)}, bf16[64,1152]{1,0:T(8,128)(2,1)S(1)}, u32[]{:S(2)}, u32[]{:S(2)}) collective-permute-start(bf16[64,1152]{1,0:T(8,128)(2,1)S(1)} %copy.23), channel_id=1, source_target_pairs={{0,2},{2,4},{4,6},{6,8},{8,10},{10,12},{12,14},{14,16},{16,18},{18... | collective-permute-start | bytes 442376 | tf_op jit(solution)/shard_map/while/body/eval_jaxpr/ppermute | solution.py:9
  376.0 8.3 %collective-permute-start.1 = (bf16[64,12,32]{0,2,1:T(8,128)(2,1)S(1)}, bf16[64,12,32]{0,2,1:T(8,128)(2,1)S(1)}, u32[]{:S(2)}, u32[]{:S(2)}) collective-permute-start(bf16[64,12,32]{0,2,1:T(8,128)(2,1)S(1)} %copy.24), channel_id=1, source_target_pairs={{0,2},{2,4},{4,6},{6,8},{8,10},{10,12},{12,14},{14,16},{16,18},{18... | collective-permute-start | bytes 147464 | tf_op jit(solution)/shard_map/while/body/eval_jaxpr/ppermute | solution.py:9
Sparse Core Ops, SparseCore 0:
  8.9 125.9 all-gather.2
  136.5 123.2 all-gather.4
where the time goes:
time: 393 us; the launch traced here: 392 us
  waiting for transfers between devices  319 us (81%)
  matrix products  43.2 us (11%)
  between operations  14.9 us (4%)
  other arithmetic  6.62 us (2%)
  blocking collectives  5.03 us (1%)
    all_gather x1, waiting for transfers between devices, on_device(): lax.all_gather(fc2_weight, 'fsdp', axis=0, tiled=True)  125 us
    all_gather x1, waiting for transfers between devices, on_device(): lax.all_gather(fc1_weight, 'fsdp', axis=1, tiled=True)  122 us
    ppermute x22, waiting for transfers between devices, from_behind(): lax.ppermute(array, axis, [(i, (i + by) % count) for i in range(count)])  70.4 us
    dot_general x1, matrix products, on_device(): jnp.dot(act, lax.all_gather(fc2_weight, 'fsdp', axis=0, tiled=True), pref...  23 us
    dot_general x12, matrix products, pair_term(): lax.dot_general(weight, units, (((0,), (0,)), ((), ())), preferred_elemen...  19.4 us
  transfers between devices with their start and end apart: 24, of which 13 were waited for; matrix products, arithmetic and copies ran while one was open for 6% of the time, Pallas kernels for 0%

commit v1 on v0

v1 whole, which is shorter than its diff:
```python
import functools

import jax
import jax.numpy as jnp
from jax import lax
from jax.experimental import pallas as pl
from jax.experimental.pallas import tpu as pltpu
from jax.sharding import PartitionSpec as P

MESH = pl.DeviceIdType.MESH
F32 = jnp.float32
BF16 = jnp.bfloat16


def layer_norm(values, gain, shift):
    centre = jnp.mean(values, axis=-1, keepdims=True)
    moved = values - centre
    spread = jnp.mean(moved * moved, axis=-1, keepdims=True)
    return moved * lax.rsqrt(spread + 1e-06) * gain + shift


def unit_rows(values):
    return values * lax.rsqrt(jnp.sum(values * values, axis=-1, keepdims=True) + 1e-06)


def mlp_kernel(
    n,
    chunk,
    tile,
    seq,
    hidden,
    keep,
    ln_gain,
    ln_bias,
    fc1_hbm,
    fc1_bias,
    fc2_hbm,
    fc2_bias,
    final_gain,
    final_bias,
    head_hbm,
    head_bias,
    unit,
    fc1,
    fc2,
    head,
    normed,
    total,
    theirs,
    back,
    parts,
    pooled,
    load_sem,
    send_sem,
    recv_sem,
    back_send,
    back_recv,
):
    dp = lax.axis_index("dp")
    me = lax.axis_index("fsdp")
    tokens = hidden.shape[0]
    units = fc1.shape[1]
    chunks = tokens // chunk
    loads = [
        pltpu.make_async_copy(src, dst, load_sem.at[i])
        for i, (src, dst) in enumerate(((fc1_hbm, fc1), (fc2_hbm, fc2), (head_hbm, head)))
    ]
    for load in loads:
        load.start()

    def ahead(by):
        return (dp, lax.rem(me + by + n, n))

    barrier = pltpu.get_barrier_semaphore()
    for by in range(1, n):
        pl.semaphore_signal(barrier, inc=1, device_id=ahead(by), device_id_type=MESH)
    pl.semaphore_wait(barrier, n - 1)

    def outward(by, c):
        rows = pl.ds(c * chunk, chunk)
        return pltpu.make_async_remote_copy(
            src_ref=normed.at[rows],
            dst_ref=theirs.at[by - 1, rows],
            send_sem=send_sem.at[by - 1, c],
            recv_sem=recv_sem.at[by - 1, c],
            device_id=ahead(by),
            device_id_type=MESH,
        )

    def homeward(by, c):
        rows = pl.ds(c * chunk, chunk)
        return pltpu.make_async_remote_copy(
            src_ref=back.at[by - 1, rows],
            dst_ref=parts.at[by - 1, rows],
            send_sem=back_send.at[by - 1, c],
            recv_sem=back_recv.at[by - 1, c],
            device_id=ahead(-by),
            device_id_type=MESH,
        )

    def norm_step(c, _):
        rows = pl.ds(pl.multiple_of(c * chunk, chunk), chunk)
        normed[rows, :] = layer_norm(
            hidden[rows, :].astype(F32), ln_gain[...], ln_bias[...]
        ).astype(BF16)
        for by in range(1, n):
            outward(by, c).start()
        return 0

    lax.fori_loop(0, chunks, norm_step, 0)
    loads[0].wait()
    loads[1].wait()

    def mlp(values):
        mixed = None
        for low in range(0, units, tile):
            high = min(low + tile, units)
            pre = jnp.dot(values, fc1[:, low:high], preferred_element_type=F32)
            act = jax.nn.gelu(pre + fc1_bias[:, low:high], approximate=True).astype(BF16)
            term = jnp.dot(act, fc2[low:high, :], preferred_element_type=F32)
            mixed = term if mixed is None else mixed + term
        return mixed

    def own_step(c, _):
        rows = pl.ds(pl.multiple_of(c * chunk, chunk), chunk)
        total[rows, :] = mlp(normed[rows, :]) + hidden[rows, :].astype(F32) + fc2_bias[...]
        return 0

    lax.fori_loop(0, chunks, own_step, 0)

    for by in range(1, n):

        def their_step(c, _):
            rows = pl.ds(pl.multiple_of(c * chunk, chunk), chunk)
            outward(by, c).wait_recv()
            back[by - 1, rows, :] = mlp(theirs[by - 1, rows, :]).astype(BF16)
            homeward(by, c).start()
            return 0

        lax.fori_loop(0, chunks, their_step, 0)

    texts = chunk // seq

    def pool_step(c, _):
        rows = pl.ds(pl.multiple_of(c * chunk, chunk), chunk)
        out = total[rows, :]
        for by in range(1, n):
            homeward(by, c).wait_recv()
            out = out + parts[by - 1, rows, :].astype(F32)
        final = layer_norm(out, final_gain[...], final_bias[...])
        kept = keep[rows, :]
        summed = jnp.sum((final * kept).reshape(texts, seq, -1), axis=1)
        count = jnp.sum(kept.reshape(texts, seq, 1), axis=1)
        pooled[pl.ds(pl.multiple_of(c * texts, texts), texts), :] = summed / count
        return 0

    lax.fori_loop(0, chunks, pool_step, 0)
    loads[2].wait()
    emb = (
        jnp.dot(pooled[...].astype(BF16), head[...], preferred_element_type=F32) + head_bias[...]
    )
    unit[...] = unit_rows(emb).astype(BF16)
    for by in range(1, n):
        for c in range(chunks):
            outward(by, c).wait_send()
            homeward(by, c).wait_send()


def score_kernel(
    n,
    count,
    unit,
    images,
    teacher,
    scale_ref,
    offset_ref,
    grad,
    every,
    weights,
    side_send,
    side_recv,
    right_send,
    right_recv,
    left_send,
    left_recv,
    twin_send,
    twin_recv,
):
    dp = lax.axis_index("dp")
    me = lax.axis_index("fsdp")
    window, group, _ = teacher.shape
    texts = unit.shape[0]
    column = count // 4
    ring = 2 * column
    core = lax.rem(dp, 2)
    y = lax.rem(dp // 2, 2)
    z = dp // 4
    place = jnp.where(y == 0, z, ring - 1 - z)

    def at_place(p, c):
        p = lax.rem(p + 2 * ring, ring)
        return jnp.where(p < column, 4 * p, 4 * (ring - 1 - p) + 2) + c

    right = at_place(place + 1, core)
    left = at_place(place - 1, core)
    twin = dp + 1 - 2 * core
    friends = [(dp, lax.rem(me + by, n)) for by in range(1, n)]
    barrier = pltpu.get_barrier_semaphore()
    for other in friends + [(right, me), (left, me), (twin, me)]:
        pl.semaphore_signal(barrier, inc=1, device_id=other, device_id_type=MESH)

    mine = pl.ds(pl.multiple_of(me * texts, texts), texts)
    every[dp, mine, :] = unit[...]
    pl.semaphore_wait(barrier, n + 2)

    def copy(block, send, recv, to):
        return pltpu.make_async_remote_copy(
            src_ref=block,
            dst_ref=block,
            send_sem=send,
            recv_sem=recv,
            device_id=to,
            device_id_type=MESH,
        )

    sent = []

    def begin(block, send, recv, to):
        out = copy(block, send, recv, to)
        out.start()
        sent.append(out)

    for by in range(1, n):
        begin(every.at[dp, mine], side_send.at[by - 1], side_recv.at[by - 1], friends[by - 1])
    picture = unit_rows(images[...].astype(F32)).astype(BF16)
    weights[...] = jnp.zeros_like(weights)
    for by in range(1, n):
        source = lax.rem(me - by + n, n)
        rows = pl.ds(pl.multiple_of(source * texts, texts), texts)
        copy(
            every.at[dp, rows], side_send.at[by - 1], side_recv.at[by - 1], friends[by - 1]
        ).wait_recv()

    to_right = ring // 2
    to_left = ring - 1 - to_right
    twins = 0

    def to_twin(block):
        begin(block, twin_send.at[twins], twin_recv.at[twins], (twin, me))

    for step in range(to_right + 1):
        if step > 0:
            block = every.at[at_place(place - step, core)]
            copy(
                block, right_send.at[step - 1], right_recv.at[step - 1], (right, me)
            ).wait_recv()
        else:
            block = every.at[dp]
        if step < to_right:
            begin(block, right_send.at[step], right_recv.at[step], (right, me))
        if step < to_left and step == 0:
            begin(block, left_send.at[step], left_recv.at[step], (left, me))
        to_twin(block)
        twins += 1
        if 0 < step <= to_left:
            block = every.at[at_place(place + step, core)]
            copy(block, left_send.at[step - 1], left_recv.at[step - 1], (left, me)).wait_recv()
            if step < to_left:
                begin(block, left_send.at[step], left_recv.at[step], (left, me))
            to_twin(block)
            twins += 1
    twins = 0
    for step in range(to_right + 1):
        sources = [place - step]
        if 0 < step <= to_left:
            sources.append(place + step)
        for source in sources:
            copy(
                every.at[at_place(source, 1 - core)],
                twin_send.at[twins],
                twin_recv.at[twins],
                (twin, me),
            ).wait_recv()
            twins += 1

    scale = scale_ref[0]
    offset = offset_ref[0]

    def weigh(s, _):
        source = lax.rem(dp - s + count, count)
        score = (
            scale
            * lax.dot_general(
                every[source], picture, (((1,), (1,)), ((), ())), preferred_element_type=F32
            )
            + offset
        )
        weight = jax.nn.sigmoid(score) - jax.nn.sigmoid(teacher[s].astype(F32))
        weights[pl.ds(pl.multiple_of(source * group, group), group), :] = weight.astype(BF16)
        return 0

    lax.fori_loop(0, window, weigh, 0)
    grad[...] = scale * lax.dot_general(
        weights[...],
        every[...].reshape(count * group, every.shape[2]),
        (((0,), (0,)), ((), ())),
        preferred_element_type=F32,
    )
    for out in sent:
        out.wait_send()


def on_device(
    hidden,
    text_ids,
    ln_gain,
    ln_bias,
    fc1_weight,
    fc1_bias,
    fc2_weight,
    fc2_bias,
    final_gain,
    final_bias,
    head_weight,
    head_bias,
    image_emb,
    teacher_logits,
    logit_scale,
    logit_bias,
):
    tokens, width = hidden.shape
    texts, seq = text_ids.shape
    units = fc1_weight.shape[1]
    group, window, pictures = teacher_logits.shape
    n = lax.axis_size("fsdp")
    count = lax.axis_size("dp")
    me = lax.axis_index("fsdp")
    chunk = min(256, tokens)
    chunks = tokens // chunk
    others = max(n - 1, 1)

    slabs = jnp.transpose(teacher_logits, (1, 0, 2))
    tiles = [slabs[0]]
    for s in range(1, window):
        tiles.append(
            lax.ppermute(slabs[s], "dp", [(i, (i + s) % count) for i in range(count)])
        )
    tiles = jnp.stack(tiles)

    keep = (text_ids != 0).astype(F32).reshape(tokens, 1)
    bias_here = lax.dynamic_slice_in_dim(fc1_bias, me * units, units).reshape(1, units)
    vmem = pl.BlockSpec(memory_space=pltpu.VMEM)
    smem = pl.BlockSpec(memory_space=pltpu.SMEM)
    hbm = pl.BlockSpec(memory_space=pl.ANY)
    dma = pltpu.SemaphoreType.DMA
    row = lambda v: v.reshape(1, -1)
    flops = 4 * n * tokens * width * units
    unit = pl.pallas_call(
        functools.partial(mlp_kernel, n, chunk, 768, seq),
        out_shape=jax.ShapeDtypeStruct((texts, width), BF16),
        in_specs=[vmem, vmem, vmem, vmem, hbm, vmem, hbm, vmem, vmem, vmem, hbm, vmem],
        out_specs=vmem,
        scratch_shapes=[
            pltpu.VMEM(fc1_weight.shape, BF16),
            pltpu.VMEM(fc2_weight.shape, BF16),
            pltpu.VMEM(head_weight.shape, BF16),
            pltpu.VMEM((tokens, width), BF16),
            pltpu.VMEM((tokens, width), F32),
            pltpu.VMEM((others, tokens, width), BF16),
            pltpu.VMEM((others, tokens, width), BF16),
            pltpu.VMEM((others, tokens, width), BF16),
            pltpu.VMEM((texts, width), F32),
            dma((3,)),
            dma((others, chunks)),
            dma((others, chunks)),
            dma((others, chunks)),
            dma((others, chunks)),
        ],
        compiler_params=pltpu.CompilerParams(
            collective_id=0, has_side_effects=True, vmem_limit_bytes=60 * 1024 * 1024
        ),
        cost_estimate=pl.CostEstimate(
            flops=flops, bytes_accessed=4 * width * units, transcendentals=n * tokens * units
        ),
    )(
        hidden,
        keep,
        row(ln_gain),
        row(ln_bias),
        fc1_weight,
        bias_here,
        fc2_weight,
        row(fc2_bias),
        row(final_gain),
        row(final_bias),
        head_weight,
        row(head_bias),
    )
    ring = count // 2
    return pl.pallas_call(
        functools.partial(score_kernel, n, count),
        out_shape=jax.ShapeDtypeStruct((pictures, width), F32),
        in_specs=[vmem, vmem, vmem, smem, smem],
        out_specs=vmem,
        scratch_shapes=[
            pltpu.VMEM((count, group, width), BF16),
            pltpu.VMEM((count * group, pictures), BF16),
            dma((others,)),
            dma((others,)),
            dma((ring,)),
            dma((ring,)),
            dma((ring,)),
            dma((ring,)),
            dma((ring,)),
            dma((ring,)),
        ],
        compiler_params=pltpu.CompilerParams(
            collective_id=1, has_side_effects=True, vmem_limit_bytes=60 * 1024 * 1024
        ),
        cost_estimate=pl.CostEstimate(
            flops=4 * count * group * pictures * width,
            bytes_accessed=2 * count * group * width,
            transcendentals=2 * window * group * pictures,
        ),
    )(unit, image_emb, tiles, logit_scale, logit_bias)


def solution(mesh):
    placed = (
        P(("dp", "fsdp"), None),
        P(("dp", "fsdp"), None),
        P(),
        P(),
        P(None, "fsdp"),
        P(),
        P("fsdp", None),
        P(),
        P(),
        P(),
        P(),
        P(),
        P(("dp", "fsdp"), None),
        P("dp", None, "fsdp"),
        P(),
        P(),
    )
    return jax.shard_map(
        on_device, mesh=mesh, in_specs=placed, out_specs=P(("dp", "fsdp"), None), check_vma=False
    )
```

time: 393 us -> 129 us (0.33)
  waiting for transfers between devices: 319 us -> 1.4 us
  Pallas kernels: 0 us -> 88.5 us
  matrix products: 43.2 us -> 0 us
  local copies, waits for them, and re-layouts: 0.5 us -> 18.5 us
  starting transfers between devices: 2.87 us -> 17.5 us
  between operations: 14.9 us -> 1.41 us
  other arithmetic: 6.62 us -> 0.7 us
  blocking collectives: 5.03 us -> 0 us
    all_gather x2 -> x0, waiting for transfers between devices: 247 us -> none  [the longest x1 125 us: on_device(): lax.all_gather(fc2_weight, 'fsdp', axis=0, tiled=True)]
    pallas_call x0 -> x2, Pallas kernels: none -> 88.5 us  [the longest x1 57.8 us: on_device(): pl.pallas_call(functools.partial(mlp_kernel, n, chunk, 768, seq), out_sha...]
    ppermute x22 -> x11, waiting for transfers between devices: 70.4 us -> 1.4 us  [on_device(): lax.ppermute(slabs[s], 'dp', [(i, (i + s) % count) for i in range(count)])]
    dot_general x14 -> x0, matrix products: 43.2 us -> none  [the longest x1 23 us: on_device(): jnp.dot(act, lax.all_gather(fc2_weight, 'fsdp', axis=0, tiled=True), pref...]
    ppermute x22 -> x11, starting transfers between devices: 2.82 us -> 17.5 us  [on_device(): lax.ppermute(slabs[s], 'dp', [(i, (i + s) % count) for i in range(count)])]
    unnamed x24 -> x25, local copies, waits for them, and re-layouts: 0.2 us -> 11.9 us
    reshape x0 -> x9, local copies, waits for them, and re-layouts: none -> 6.5 us  [the longest x6 4.96 us: on_device(): row = lambda v: v.reshape(1, -1)]
    reduce_sum x6 -> x0, other arithmetic: 6.42 us -> none  [the longest x2 3.91 us: layer_norm(): spread = jnp.mean((values - centre) ** 2, axis=-1, keepdims=True)]
  transfers between devices with their start and end apart: 24 -> 11, of which waited for: 13 -> 2; matrix products, arithmetic and copies ran while one was open for 6% -> 12% of each run, Pallas kernels for 0% -> 45%
where the time goes in v1:
time: 129 us; the launch traced here: 128 us
  Pallas kernels  88.5 us (69%)
  local copies, waits for them, and re-layouts  18.5 us (14%)
  starting transfers between devices  17.5 us (14%)
  between operations  1.41 us (1%)
  waiting for transfers between devices  1.4 us (1%)
    pallas_call x1, Pallas kernels, on_device(): pl.pallas_call(functools.partial(mlp_kernel, n, chunk, 768, seq), out_sha...  57.8 us
    pallas_call x1, Pallas kernels, on_device(): pl.pallas_call(functools.partial(score_kernel, n, count), out_shape=jax.S...  30.8 us
    ppermute x11, starting transfers between devices, on_device(): lax.ppermute(slabs[s], 'dp', [(i, (i + s) % count) for i in range(count)])  17.5 us
    unnamed x25, local copies, waits for them, and re-layouts  11.9 us
    reshape x6, local copies, waits for them, and re-layouts, on_device(): row = lambda v: v.reshape(1, -1)  4.96 us
  transfers between devices with their start and end apart: 11, of which 2 were waited for; matrix products, arithmetic and copies ran while one was open for 12% of the time, Pallas kernels for 45%

profile of v1, /device:TPU:0, one launch (start us, length us, event | category | flops | bytes accessed | tf_op | source)
XLA Modules:
  0.0 128.0 jit_solution(8911659518300185787)
XLA Ops:
  0.0 1.0 copy.23
  1.1 0.5 collective-permute-start
  1.6 2.6 %collective-permute-start.1 = (bf16[64,32]{1,0:T(8,128)(2,1)S(1)}, bf16[64,32]{1,0:T(8,128)(2,1)S(1)}, u32[]{:S(2)}, u32[]{:S(2)}) collective-permute-start(bf16[64,32]{1,0:T(8,128)(2,1)S(1)} %get-tuple-element.14), channel_id=1, source_target_pairs={{0,4},{2,6},{4,8},{6,10},{8,12},{10,14},{12,16},{14,18},{16,20},{1... | collective-permute-start | bytes 12296 | tf_op jit(solution)/shard_map/ppermute | solution.py:346
  4.1 2.4 %collective-permute-start.2 = (bf16[64,32]{1,0:T(8,128)(2,1)S(1)}, bf16[64,32]{1,0:T(8,128)(2,1)S(1)}, u32[]{:S(2)}, u32[]{:S(2)}) collective-permute-start(bf16[64,32]{1,0:T(8,128)(2,1)S(1)} %get-tuple-element.13), channel_id=1, source_target_pairs={{0,6},{2,8},{4,10},{6,12},{8,14},{10,16},{12,18},{14,20},{16,22},{... | collective-permute-start | bytes 12296 | tf_op jit(solution)/shard_map/ppermute | solution.py:346
  6.6 1.6 %collective-permute-start.3 = (bf16[64,32]{1,0:T(8,128)(2,1)S(1)}, bf16[64,32]{1,0:T(8,128)(2,1)S(1)}, u32[]{:S(2)}, u32[]{:S(2)}) collective-permute-start(bf16[64,32]{1,0:T(8,128)(2,1)S(1)} %get-tuple-element.12), channel_id=1, source_target_pairs={{0,8},{2,10},{4,12},{6,14},{8,16},{10,18},{12,20},{14,22},{16,24},... | collective-permute-start | bytes 12296 | tf_op jit(solution)/shard_map/ppermute | solution.py:346
  8.1 0.2 collective-permute-start.4
  8.3 0.7 compare_convert_fusion
  9.0 0.1 copy.20
  9.1 0.9 reshape.37.keep
  10.0 1.3 %reshape.28.ln_gain = f32[1,1152]{1,0:T(1,128)} reshape(f32[1152]{0:T(1024)} %param.18) | data formatting | bytes 9216 | tf_op jit(solution)/shard_map/reshape | solution.py:356
  11.2 1.3 %reshape.29.ln_bias = f32[1,1152]{1,0:T(1,128)} reshape(f32[1152]{0:T(1024)} %param.19) | data formatting | bytes 9216 | tf_op jit(solution)/shard_map/reshape | solution.py:356
  12.5 0.0 copy-start.4
  12.5 0.0 copy-start
  12.5 0.0 copy-start.1
  12.6 0.0 copy-start.2
  12.6 0.0 copy-start.3
  12.6 8.5 %copy.22.fc1_hbm = bf16[1152,2152]{1,0:T(8,128)(2,1)} copy(bf16[1152,2152]{0,1:T(8,128)(2,1)} %param.20) | data formatting | bytes 9916416 | tf_op args[4]
  21.0 0.0 copy-done.4
  21.0 0.1 dynamic_slice.3
  21.1 0.6 reshape.30.fc1_bias
  21.7 0.0 copy-done
  21.7 0.6 reshape.31.fc2_bias
  22.3 0.0 copy-done.1
  22.3 0.6 reshape.32.final_gain
  22.9 0.0 copy-done.2
  22.9 0.6 reshape.33.final_bias
  23.5 0.0 copy-done.3
  23.5 0.6 reshape.34.head_bias
  24.1 57.8 %shard_map.154.unit = bf16[32,1152]{1,0:T(8,128)(2,1)} custom-call(bf16[512,1152]{1,0:T(8,128)(2,1)} %hidden.1, f32[512,1]{1,0:T(8,128)} %reshape.37.keep, f32[1,1152]{1,0:T(1,128)} %reshape.28.ln_gain, f32[1,1152]{1,0:T(1,128)} %reshape.29.ln_bias, bf16[1152,2152]{1,0:T(8,128)(2,1)} %copy.22.fc1_hbm, f32[1,2152]{1,0:T(1,128)} %reshape.30.fc1_bias, ...), custom_call_target="tpu_custom_call" | custom-call | flops 10154409984 | bytes 9916416 | tf_op jit(solution)/shard_map/pallas_call | solution.py:358
  83.2 0.0 collective-permute-done
  83.2 0.1 collective-permute-start.5
  83.3 0.0 collective-permute-done.1
  83.3 3.1 %collective-permute-start.6 = (bf16[64,32]{1,0:T(8,128)(2,1)S(1)}, bf16[64,32]{1,0:T(8,128)(2,1)S(1)}, u32[]{:S(2)}, u32[]{:S(2)}) collective-permute-start(bf16[64,32]{1,0:T(8,128)(2,1)S(1)} %get-tuple-element.9), channel_id=1, source_target_pairs={{0,14},{2,16},{4,18},{6,20},{8,22},{10,24},{12,26},{14,28},{16,30}... | collective-permute-start | bytes 12296 | tf_op jit(solution)/shard_map/ppermute | solution.py:346
  86.4 0.0 collective-permute-done.2
  86.4 1.5 %collective-permute-start.7 = (bf16[64,32]{1,0:T(8,128)(2,1)S(1)}, bf16[64,32]{1,0:T(8,128)(2,1)S(1)}, u32[]{:S(2)}, u32[]{:S(2)}) collective-permute-start(bf16[64,32]{1,0:T(8,128)(2,1)S(1)} %get-tuple-element.8), channel_id=1, source_target_pairs={{0,16},{2,18},{4,20},{6,22},{8,24},{10,26},{12,28},{14,30},{16,0},... | collective-permute-start | bytes 12296 | tf_op jit(solution)/shard_map/ppermute | solution.py:346
  87.9 0.0 collective-permute-done.3
  87.9 1.2 collective-permute-start.8
  89.2 0.0 collective-permute-done.4
  89.2 1.2 collective-permute-start.9
  90.4 0.0 collective-permute-done.5
  90.4 3.1 %collective-permute-start.10 = (bf16[64,32]{1,0:T(8,128)(2,1)S(1)}, bf16[64,32]{1,0:T(8,128)(2,1)S(1)}, u32[]{:S(2)}, u32[]{:S(2)}) collective-permute-start(bf16[64,32]{1,0:T(8,128)(2,1)S(1)} %get-tuple-element.5), channel_id=1, source_target_pairs={{0,22},{2,24},{4,26},{6,28},{8,30},{10,0},{12,2},{14,4},{16,6},{18... | collective-permute-start | bytes 12296 | tf_op jit(solution)/shard_map/ppermute | solution.py:346
  93.5 0.0 collective-permute-done.6
  93.5 0.0 collective-permute-done.7
  93.6 0.0 collective-permute-done.8
  93.6 0.2 collective-permute-done.9
  93.8 1.1 collective-permute-done.10
  95.0 0.0 copy-start.5
  95.0 0.7 copy-done.5
  95.7 30.8 %shard_map.155 = f32[32,1152]{1,0:T(8,128)} custom-call(bf16[32,1152]{1,0:T(8,128)(2,1)} %shard_map.154.unit, bf16[32,1152]{1,0:T(8,128)(2,1)} %images.1, bf16[12,64,32]{2,1,0:T(8,128)(2,1)} %copy-done.5, f32[1]{0:T(128)S(6)} %copy.36.scale_ref, f32[1]{0:T(128)S(6)} %copy.37.offset_ref), custom_call_target="tpu_custom_call" | custom-call | flops 150994944 | bytes 2359296 | tf_op jit(solution)/shard_map/pallas_call | solution.py:400
  126.4 1.6 %copy.38 = f32[32,1152]{1,0:T(8,128)} copy(f32[32,1152]{1,0:T(8,128)} %shard_map.155) | data formatting | bytes 294912
  (12 shorter events, 0.1 us)
Async XLA Ops:
  1.1 82.1 %collective-permute-start = (bf16[64,32]{1,0:T(8,128)(2,1)S(1)}, bf16[64,32]{1,0:T(8,128)(2,1)S(1)}, u32[]{:S(2)}, u32[]{:S(2)}) collective-permute-start(bf16[64,32]{1,0:T(8,128)(2,1)S(1)} %get-tuple-element.15), channel_id=1, source_target_pairs={{0,2},{2,4},{4,6},{6,8},{8,10},{10,12},{12,14},{14,16},{16,18},{18... | collective-permute-start | bytes 12296 | tf_op jit(solution)/shard_map/ppermute | solution.py:346
  1.6 81.7 %collective-permute-start.1 = (bf16[64,32]{1,0:T(8,128)(2,1)S(1)}, bf16[64,32]{1,0:T(8,128)(2,1)S(1)}, u32[]{:S(2)}, u32[]{:S(2)}) collective-permute-start(bf16[64,32]{1,0:T(8,128)(2,1)S(1)} %get-tuple-element.14), channel_id=1, source_target_pairs={{0,4},{2,6},{4,8},{6,10},{8,12},{10,14},{12,16},{14,18},{16,20},{1... | collective-permute-start | bytes 12296 | tf_op jit(solution)/shard_map/ppermute | solution.py:346
  4.1 82.3 %collective-permute-start.2 = (bf16[64,32]{1,0:T(8,128)(2,1)S(1)}, bf16[64,32]{1,0:T(8,128)(2,1)S(1)}, u32[]{:S(2)}, u32[]{:S(2)}) collective-permute-start(bf16[64,32]{1,0:T(8,128)(2,1)S(1)} %get-tuple-element.13), channel_id=1, source_target_pairs={{0,6},{2,8},{4,10},{6,12},{8,14},{10,16},{12,18},{14,20},{16,22},{... | collective-permute-start | bytes 12296 | tf_op jit(solution)/shard_map/ppermute | solution.py:346
  6.6 81.4 %collective-permute-start.3 = (bf16[64,32]{1,0:T(8,128)(2,1)S(1)}, bf16[64,32]{1,0:T(8,128)(2,1)S(1)}, u32[]{:S(2)}, u32[]{:S(2)}) collective-permute-start(bf16[64,32]{1,0:T(8,128)(2,1)S(1)} %get-tuple-element.12), channel_id=1, source_target_pairs={{0,8},{2,10},{4,12},{6,14},{8,16},{10,18},{12,20},{14,22},{16,24},... | collective-permute-start | bytes 12296 | tf_op jit(solution)/shard_map/ppermute | solution.py:346
  8.1 81.0 %collective-permute-start.4 = (bf16[64,32]{1,0:T(8,128)(2,1)S(1)}, bf16[64,32]{1,0:T(8,128)(2,1)S(1)}, u32[]{:S(2)}, u32[]{:S(2)}) collective-permute-start(bf16[64,32]{1,0:T(8,128)(2,1)S(1)} %get-tuple-element.11), channel_id=1, source_target_pairs={{0,10},{2,12},{4,14},{6,16},{8,18},{10,20},{12,22},{14,24},{16,26}... | collective-permute-start | bytes 12296 | tf_op jit(solution)/shard_map/ppermute | solution.py:346
  12.5 8.5 %copy-start.4 = (f32[4304]{0:T(1024)S(1)}, f32[4304]{0:T(1024)}, u32[]{:S(2)}) copy-start(f32[4304]{0:T(1024)} %param.21) | copy-start | bytes 51652
  12.5 9.2 %copy-start = (f32[1152]{0:T(1024)S(1)}, f32[1152]{0:T(1024)}, u32[]{:S(2)}) copy-start(f32[1152]{0:T(1024)} %param.23) | copy-start | bytes 13828
  12.5 9.8 %copy-start.1 = (f32[1152]{0:T(1024)S(1)}, f32[1152]{0:T(1024)}, u32[]{:S(2)}) copy-start(f32[1152]{0:T(1024)} %param.24) | copy-start | bytes 13828
  12.6 10.4 %copy-start.2 = (f32[1152]{0:T(1024)S(1)}, f32[1152]{0:T(1024)}, u32[]{:S(2)}) copy-start(f32[1152]{0:T(1024)} %param.25) | copy-start | bytes 13828
  12.6 11.0 %copy-start.3 = (f32[1152]{0:T(1024)S(1)}, f32[1152]{0:T(1024)}, u32[]{:S(2)}) copy-start(f32[1152]{0:T(1024)} %param.27) | copy-start | bytes 13828
  83.2 7.2 %collective-permute-start.5 = (bf16[64,32]{1,0:T(8,128)(2,1)S(1)}, bf16[64,32]{1,0:T(8,128)(2,1)S(1)}, u32[]{:S(2)}, u32[]{:S(2)}) collective-permute-start(bf16[64,32]{1,0:T(8,128)(2,1)S(1)} %get-tuple-element.10), channel_id=1, source_target_pairs={{0,12},{2,14},{4,16},{6,18},{8,20},{10,22},{12,24},{14,26},{16,28}... | collective-permute-start | bytes 12296 | tf_op jit(solution)/shard_map/ppermute | solution.py:346
  83.3 10.3 %collective-permute-start.6 = (bf16[64,32]{1,0:T(8,128)(2,1)S(1)}, bf16[64,32]{1,0:T(8,128)(2,1)S(1)}, u32[]{:S(2)}, u32[]{:S(2)}) collective-permute-start(bf16[64,32]{1,0:T(8,128)(2,1)S(1)} %get-tuple-element.9), channel_id=1, source_target_pairs={{0,14},{2,16},{4,18},{6,20},{8,22},{10,24},{12,26},{14,28},{16,30}... | collective-permute-start | bytes 12296 | tf_op jit(solution)/shard_map/ppermute | solution.py:346
  86.4 7.1 %collective-permute-start.7 = (bf16[64,32]{1,0:T(8,128)(2,1)S(1)}, bf16[64,32]{1,0:T(8,128)(2,1)S(1)}, u32[]{:S(2)}, u32[]{:S(2)}) collective-permute-start(bf16[64,32]{1,0:T(8,128)(2,1)S(1)} %get-tuple-element.8), channel_id=1, source_target_pairs={{0,16},{2,18},{4,20},{6,22},{8,24},{10,26},{12,28},{14,30},{16,0},... | collective-permute-start | bytes 12296 | tf_op jit(solution)/shard_map/ppermute | solution.py:346
  87.9 5.6 %collective-permute-start.8 = (bf16[64,32]{1,0:T(8,128)(2,1)S(1)}, bf16[64,32]{1,0:T(8,128)(2,1)S(1)}, u32[]{:S(2)}, u32[]{:S(2)}) collective-permute-start(bf16[64,32]{1,0:T(8,128)(2,1)S(1)} %get-tuple-element.7), channel_id=1, source_target_pairs={{0,18},{2,20},{4,22},{6,24},{8,26},{10,28},{12,30},{14,0},{16,2},{... | collective-permute-start | bytes 12296 | tf_op jit(solution)/shard_map/ppermute | solution.py:346
  89.2 4.6 %collective-permute-start.9 = (bf16[64,32]{1,0:T(8,128)(2,1)S(1)}, bf16[64,32]{1,0:T(8,128)(2,1)S(1)}, u32[]{:S(2)}, u32[]{:S(2)}) collective-permute-start(bf16[64,32]{1,0:T(8,128)(2,1)S(1)} %get-tuple-element.6), channel_id=1, source_target_pairs={{0,20},{2,22},{4,24},{6,26},{8,28},{10,30},{12,0},{14,2},{16,4},{1... | collective-permute-start | bytes 12296 | tf_op jit(solution)/shard_map/ppermute | solution.py:346
  90.4 4.6 %collective-permute-start.10 = (bf16[64,32]{1,0:T(8,128)(2,1)S(1)}, bf16[64,32]{1,0:T(8,128)(2,1)S(1)}, u32[]{:S(2)}, u32[]{:S(2)}) collective-permute-start(bf16[64,32]{1,0:T(8,128)(2,1)S(1)} %get-tuple-element.5), channel_id=1, source_target_pairs={{0,22},{2,24},{4,26},{6,28},{8,30},{10,0},{12,2},{14,4},{16,6},{18... | collective-permute-start | bytes 12296 | tf_op jit(solution)/shard_map/ppermute | solution.py:346
  95.0 0.7 copy-start.5

commit v2 on v0

v2 whole, which is shorter than its diff:
```python
import functools

import jax
import jax.numpy as jnp
from jax import lax
from jax.experimental import pallas as pl
from jax.experimental.pallas import tpu as pltpu
from jax.sharding import PartitionSpec as P

MESH = pl.DeviceIdType.MESH
F32 = jnp.float32
BF16 = jnp.bfloat16


def layer_norm(values, gain, shift):
    centre = jnp.mean(values, axis=-1, keepdims=True)
    moved = values - centre
    spread = jnp.mean(moved * moved, axis=-1, keepdims=True)
    return moved * lax.rsqrt(spread + 1e-06) * gain + shift


def unit_rows(values):
    return values * lax.rsqrt(jnp.sum(values * values, axis=-1, keepdims=True) + 1e-06)


def tower_kernel(
    n,
    count,
    tile,
    hidden,
    text_ids,
    ln_gain,
    ln_bias,
    fc1_hbm,
    fc1_bias,
    fc2_hbm,
    fc2_bias,
    final_gain,
    final_bias,
    head_hbm,
    head_bias,
    images,
    slabs,
    scale_ref,
    offset_ref,
    grad,
    fc1,
    fc2,
    head,
    normed,
    total,
    theirs,
    parts,
    every,
    tiles,
    load_sem,
    send_sem,
    recv_sem,
    back_send,
    back_recv,
    teach_send,
    teach_recv,
    side_send,
    side_recv,
    right_send,
    right_recv,
    left_send,
    left_recv,
    twin_send,
    twin_recv,
):
    dp = lax.axis_index("dp")
    me = lax.axis_index("fsdp")
    tokens, width = hidden.shape
    texts, seq = text_ids.shape
    units = fc1.shape[0]
    window = slabs.shape[0]
    phases, _, rows_here, _ = every.shape
    chunk = tokens // phases
    half = chunk // 2
    slots = texts // phases
    loads = [
        pltpu.make_async_copy(src, dst, load_sem.at[i])
        for i, (src, dst) in enumerate(((fc1_hbm, fc1), (fc2_hbm, fc2), (head_hbm, head)))
    ]
    for load in loads:
        load.start()

    column = count // 4
    ring = 2 * column
    core = lax.rem(dp, 2)
    y = lax.rem(dp // 2, 2)
    z = dp // 4
    place = jnp.where(y == 0, z, ring - 1 - z)

    def at_place(p, c):
        p = lax.rem(p + 2 * ring, ring)
        return jnp.where(p < column, 4 * p, 4 * (ring - 1 - p) + 2) + c

    right = at_place(place + 1, core)
    left = at_place(place - 1, core)
    twin = dp + 1 - 2 * core

    def ahead(by):
        return (dp, lax.rem(me + by + n, n))

    def later(s):
        return lax.rem(dp + s + count, count)

    tiles[...] = jnp.zeros_like(tiles)
    barrier = pltpu.get_barrier_semaphore()
    near = [ahead(by) for by in range(1, n)] + [(right, me), (left, me), (twin, me)]
    for other in near:
        pl.semaphore_signal(barrier, inc=1, device_id=other, device_id_type=MESH)

    def greet(s, _):
        pl.semaphore_signal(barrier, inc=1, device_id=(later(-s), me), device_id_type=MESH)
        return 0

    lax.fori_loop(1, window, greet, 0)

    def copy(src, dst, send, recv, to):
        return pltpu.make_async_remote_copy(
            src_ref=src, dst_ref=dst, send_sem=send, recv_sem=recv, device_id=to, device_id_type=MESH
        )

    def outward(by, c):
        rows = pl.ds(c * chunk, chunk)
        return copy(
            normed.at[rows],
            theirs.at[by - 1, rows],
            send_sem.at[by - 1, c],
            recv_sem.at[by - 1, c],
            ahead(by),
        )

    def homeward(by, c):
        rows = pl.ds(c * half, half)
        return copy(
            theirs.at[by - 1, rows],
            parts.at[by - 1, rows],
            back_send.at[by - 1, c],
            back_recv.at[by - 1, c],
            ahead(-by),
        )

    def lesson(s, block):
        return copy(slabs.at[s], tiles.at[block], teach_send.at[s], teach_recv.at[s], (later(s), me))

    def normalise(c):
        rows = pl.ds(c * chunk, chunk)
        normed[rows, :] = layer_norm(
            hidden[rows, :].astype(F32), ln_gain[...], ln_bias[...]
        ).astype(BF16)

    normalise(0)
    pl.semaphore_wait(barrier, n + 2 + window - 1)
    for c in range(phases):
        if c > 0:
            normalise(c)
        for by in range(1, n):
            outward(by, c).start()

    def teach(s, _):
        lesson(s, dp).start()
        return 0

    lax.fori_loop(1, window, teach, 0)
    tiles[dp] = slabs[0]
    picture = unit_rows(images[...].astype(F32)).astype(BF16)
    loads[0].wait()
    loads[1].wait()

    def mlp(values):
        mixed = None
        for low in range(0, units, tile):
            high = min(low + tile, units)
            pre = lax.dot_general(
                values, fc1[low:high, :], (((1,), (1,)), ((), ())), preferred_element_type=F32
            )
            bias = fc1_bias[pl.ds(me, 1), low:high]
            act = jax.nn.gelu(pre + bias, approximate=True).astype(BF16)
            term = jnp.dot(act, fc2[low:high, :], preferred_element_type=F32)
            mixed = term if mixed is None else mixed + term
        return mixed

    def own_step(c, _):
        rows = pl.ds(pl.multiple_of(c * chunk, chunk), chunk)
        total[rows, :] = mlp(normed[rows, :]) + hidden[rows, :].astype(F32) + fc2_bias[...]
        return 0

    lax.fori_loop(0, phases, own_step, 0)

    def their_step(c, _):
        rows = pl.ds(pl.multiple_of(c * chunk, chunk), chunk)
        for by in range(1, n):
            outward(by, c).wait_recv()

        def one(slot, _):
            theirs[slot, rows, :] = mlp(theirs[slot, rows, :]).astype(BF16)
            return 0

        lax.fori_loop(0, n - 1, one, 0)
        for by in range(1, n):
            homeward(by, 2 * c).start()

        @pl.when(c < phases - 1)
        def _():
            for by in range(1, n):
                homeward(by, 2 * c + 1).start()

        return 0

    lax.fori_loop(0, phases, their_step, 0)
    loads[2].wait()

    def embed(c):
        rows = pl.ds(c * chunk, chunk)
        out = total[rows, :]
        for by in range(1, n):
            homeward(by, 2 * c).wait_recv()
            homeward(by, 2 * c + 1).wait_recv()
            out = out + parts[by - 1, rows, :].astype(F32)
        final = layer_norm(out, final_gain[...], final_bias[...])
        kept = (text_ids[pl.ds(c * slots, slots), :] != 0).astype(F32)
        summed = jnp.sum(final.reshape(slots, seq, width) * kept[:, :, None], axis=1)
        pooled = summed / jnp.sum(kept, axis=1, keepdims=True)
        emb = (
            jnp.dot(pooled.astype(BF16), head[...], preferred_element_type=F32) + head_bias[...]
        )
        return unit_rows(emb).astype(BF16)

    sent = []

    def begin(block, send, recv, to):
        out = copy(block, block, send, recv, to)
        out.start()
        sent.append(out)

    def part(h, f):
        return every.at[h, dp, pl.ds(pl.multiple_of(f * slots, slots), slots)]

    def exchange(h):
        every[h, dp, pl.ds(pl.multiple_of(me * slots, slots), slots), :] = embed(h)
        for by in range(1, n):
            begin(part(h, me), side_send.at[h, by - 1], side_recv.at[h, by - 1], ahead(by))

    to_right = ring // 2
    to_left = ring - 1 - to_right

    def circulate(h):
        for by in range(1, n):
            block = part(h, lax.rem(me - by + n, n))
            copy(block, block, side_send.at[h, by - 1], side_recv.at[h, by - 1], ahead(by)).wait_recv()
        twins = 0
        for step in range(to_right + 1):
            block = every.at[h, at_place(place - step, core)]
            if step > 0:
                copy(
                    block, block, right_send.at[h, step - 1], right_recv.at[h, step - 1], (right, me)
                ).wait_recv()
            if step < to_right:
                begin(block, right_send.at[h, step], right_recv.at[h, step], (right, me))
            if step == 0 and to_left > 0:
                begin(block, left_send.at[h, 0], left_recv.at[h, 0], (left, me))
            begin(block, twin_send.at[h, twins], twin_recv.at[h, twins], (twin, me))
            twins += 1
            if 0 < step <= to_left:
                block = every.at[h, at_place(place + step, core)]
                copy(
                    block, block, left_send.at[h, step - 1], left_recv.at[h, step - 1], (left, me)
                ).wait_recv()
                if step < to_left:
                    begin(block, left_send.at[h, step], left_recv.at[h, step], (left, me))
                begin(block, twin_send.at[h, twins], twin_recv.at[h, twins], (twin, me))
                twins += 1
        twins = 0
        for step in range(to_right + 1):
            sources = [place - step]
            if 0 < step <= to_left:
                sources.append(place + step)
            for source in sources:
                block = every.at[h, at_place(source, 1 - core)]
                copy(
                    block, block, twin_send.at[h, twins], twin_recv.at[h, twins], (twin, me)
                ).wait_recv()
                twins += 1

    scale = scale_ref[0]
    offset = offset_ref[0]
    pictures = images.shape[0]
    span = (count, rows_here, pictures)
    behind = dp - lax.broadcasted_iota(jnp.int32, span, 0)
    met = jnp.where(behind < 0, behind + count, behind) < window

    def gradient(h):
        group = every[h].reshape(count * rows_here, width)
        dots = lax.dot_general(
            group, picture, (((1,), (1,)), ((), ())), preferred_element_type=F32
        )
        score = (scale * dots + offset).reshape(span)
        gap = jax.nn.sigmoid(score) - jax.nn.sigmoid(tiles[:, h].astype(F32))
        weight = jnp.where(met, gap, 0.0).astype(BF16).reshape(count * rows_here, pictures)
        return lax.dot_general(
            weight, group, (((0,), (0,)), ((), ())), preferred_element_type=F32
        )

    def taught(s, _):
        lesson(s, later(-s)).wait_recv()
        return 0

    for h in range(phases):
        exchange(h)
        if h == 0:
            for by in range(1, n):
                homeward(by, 2 * phases - 1).start()
        circulate(h)
        if h == 0:
            lax.fori_loop(1, window, taught, 0)
            grad[...] = gradient(h)
        else:
            grad[...] += gradient(h)
    grad[...] = scale * grad[...]

    def told(s, _):
        lesson(s, dp).wait_send()
        return 0

    lax.fori_loop(1, window, told, 0)
    for by in range(1, n):
        for c in range(phases):
            outward(by, c).wait_send()
        for c in range(2 * phases):
            homeward(by, c).wait_send()
    for out in sent:
        out.wait_send()


def on_device(
    hidden,
    text_ids,
    ln_gain,
    ln_bias,
    fc1_weight,
    fc1_bias,
    fc2_weight,
    fc2_bias,
    final_gain,
    final_bias,
    head_weight,
    head_bias,
    image_emb,
    teacher_logits,
    logit_scale,
    logit_bias,
):
    tokens, width = hidden.shape
    texts, seq = text_ids.shape
    units = fc1_weight.shape[1]
    group, window, pictures = teacher_logits.shape
    n = lax.axis_size("fsdp")
    count = lax.axis_size("dp")
    phases = 2
    slots = texts // phases
    others = max(n - 1, 1)

    slabs = jnp.transpose(
        teacher_logits.reshape(n, phases, slots, window, pictures), (3, 1, 0, 2, 4)
    ).reshape(window, phases, n * slots, pictures)
    vmem = pl.BlockSpec(memory_space=pltpu.VMEM)
    smem = pl.BlockSpec(memory_space=pltpu.SMEM)
    hbm = pl.BlockSpec(memory_space=pl.ANY)
    dma = pltpu.SemaphoreType.DMA
    ring = count // 2
    return pl.pallas_call(
        functools.partial(tower_kernel, n, count, 768),
        out_shape=jax.ShapeDtypeStruct((pictures, width), F32),
        in_specs=[vmem] * 4 + [hbm, vmem, hbm, vmem, vmem, vmem, hbm, vmem, vmem, vmem, smem, smem],
        out_specs=vmem,
        scratch_shapes=[
            pltpu.VMEM((units, width), BF16),
            pltpu.VMEM(fc2_weight.shape, BF16),
            pltpu.VMEM(head_weight.shape, BF16),
            pltpu.VMEM((tokens, width), BF16),
            pltpu.VMEM((tokens, width), F32),
            pltpu.VMEM((others, tokens, width), BF16),
            pltpu.VMEM((others, tokens, width), BF16),
            pltpu.VMEM((phases, count, n * slots, width), BF16),
            pltpu.VMEM((count, phases, n * slots, pictures), BF16),
            dma((3,)),
            dma((others, phases)),
            dma((others, phases)),
            dma((others, 2 * phases)),
            dma((others, 2 * phases)),
            dma((window,)),
            dma((window,)),
            dma((phases, others)),
            dma((phases, others)),
        ]
        + [dma((phases, ring))] * 6,
        compiler_params=pltpu.CompilerParams(
            collective_id=0, has_side_effects=True, vmem_limit_bytes=62 * 1024 * 1024
        ),
        cost_estimate=pl.CostEstimate(
            flops=4 * n * tokens * width * units,
            bytes_accessed=4 * width * units,
            transcendentals=n * tokens * units,
        ),
    )(
        hidden,
        text_ids,
        ln_gain,
        ln_bias,
        fc1_weight.T,
        fc1_bias.reshape(n, units),
        fc2_weight,
        fc2_bias,
        final_gain,
        final_bias,
        head_weight,
        head_bias,
        image_emb,
        slabs,
        logit_scale,
        logit_bias,
    )


def solution(mesh):
    placed = (
        P(("dp", "fsdp"), None),
        P(("dp", "fsdp"), None),
        P(),
        P(),
        P(None, "fsdp"),
        P(),
        P("fsdp", None),
        P(),
        P(),
        P(),
        P(),
        P(),
        P(("dp", "fsdp"), None),
        P("dp", None, "fsdp"),
        P(),
        P(),
    )
    return jax.shard_map(
        on_device, mesh=mesh, in_specs=placed, out_specs=P(("dp", "fsdp"), None), check_vma=False
    )
```

time: 393 us -> 99 us (0.25)
  waiting for transfers between devices: 319 us -> 0 us
  Pallas kernels: 0 us -> 90.1 us
  matrix products: 43.2 us -> 0 us
  between operations: 14.9 us -> 1.31 us
  other arithmetic: 6.62 us -> 0 us
  local copies, waits for them, and re-layouts: 0.5 us -> 6.08 us
  blocking collectives: 5.03 us -> 0 us
    all_gather x2 -> x0, waiting for transfers between devices: 247 us -> none  [the longest x1 125 us: on_device(): lax.all_gather(fc2_weight, 'fsdp', axis=0, tiled=True)]
    pallas_call x0 -> x1, Pallas kernels: none -> 90.1 us  [on_device(): pl.pallas_call(functools.partial(tower_kernel, n, count, 768), out_shape=...]
    ppermute x22 -> x0, waiting for transfers between devices: 70.4 us -> none  [from_behind(): lax.ppermute(array, axis, [(i, (i + by) % count) for i in range(count)])]
    dot_general x14 -> x0, matrix products: 43.2 us -> none  [the longest x1 23 us: on_device(): jnp.dot(act, lax.all_gather(fc2_weight, 'fsdp', axis=0, tiled=True), pref...]
    reduce_sum x6 -> x0, other arithmetic: 6.42 us -> none  [the longest x2 3.91 us: layer_norm(): spread = jnp.mean((values - centre) ** 2, axis=-1, keepdims=True)]
    all_gather x1 -> x0, blocking collectives: 5.03 us -> none  [on_device(): group_units = lax.all_gather(text_unit, 'fsdp', axis=0, tiled=True)]
  transfers between devices with their start and end apart: 24 -> 0, of which waited for: 13 -> 0; matrix products, arithmetic and copies ran while one was open for 6% -> 0% of each run, Pallas kernels for 0% -> 0%
where the time goes in v2:
time: 99 us; the launch traced here: 97.5 us
  Pallas kernels  90.1 us (91%)
  local copies, waits for them, and re-layouts  6.08 us (6%)
  between operations  1.31 us (1%)
    pallas_call x1, Pallas kernels, on_device(): pl.pallas_call(functools.partial(tower_kernel, n, count, 768), out_shape=...  90.1 us
    unnamed x3, local copies, waits for them, and re-layouts  3.98 us

profile of v2, /device:TPU:0, one launch (start us, length us, event | category | flops | bytes accessed | tf_op | source)
XLA Modules:
  0.0 97.5 jit_solution(2851775919310896653)
XLA Ops:
  0.0 1.0 %copy.19 = bf16[64,12,32]{2,0,1:T(8,128)(2,1)S(1)} copy(bf16[64,12,32]{0,2,1:T(8,128)(2,1)} %param.29) | data formatting | bytes 98304 | tf_op args[13]
  1.0 0.7 copy.20
  1.7 1.4 %reshape.9.fc1_bias = f32[2,2152]{1,0:T(2,128)} reshape(f32[4304]{0:T(1024)} %param.21) | data formatting | bytes 34432 | tf_op jit(solution)/shard_map/reshape | solution.py:415
  3.1 1.4 %copy.21.text_ids = s32[32,16]{1,0:T(8,128)} copy(s32[32,16]{0,1:T(8,128)} %param.17) | data formatting | bytes 4096 | tf_op args[1]
  5.8 90.1 %shard_map.154 = f32[32,1152]{1,0:T(8,128)} custom-call(bf16[512,1152]{1,0:T(8,128)(2,1)} %hidden.1, s32[32,16]{1,0:T(8,128)} %copy.21.text_ids, f32[1152]{0:T(1024)} %ln_gain.1, f32[1152]{0:T(1024)} %ln_bias.1, bf16[2152,1152]{1,0:T(8,128)(2,1)} %bitcast.7, f32[2,2152]{1,0:T(2,128)} %reshape.9.fc1_bias, bf16[2152,1152]{1,0:T(8,128)(2,1)} %fc2_hbm.1, ...), custom_call_target="tpu_custom_call" | custom-call | flops 10154409984 | bytes 9916416 | tf_op jit(solution)/shard_map/pallas_call | solution.py:375
  95.9 1.6 %copy.25 = f32[32,1152]{1,0:T(8,128)} copy(f32[32,1152]{1,0:T(8,128)} %shard_map.154) | data formatting | bytes 294912

commit v3 on v2

--- a/solution.py
+++ b/solution.py
@@ -40,10 +40,13 @@
     head_hbm,
     head_bias,
     images,
-    slabs,
+    teacher,
     scale_ref,
     offset_ref,
     grad,
+    slabs,
+    bias,
+    kept_rows,
     fc1,
     fc2,
     head,
@@ -72,12 +75,13 @@
     dp = lax.axis_index("dp")
     me = lax.axis_index("fsdp")
     tokens, width = hidden.shape
-    texts, seq = text_ids.shape
+    seq, texts = text_ids.shape
     units = fc1.shape[0]
     window = slabs.shape[0]
     phases, _, rows_here, _ = every.shape
     chunk = tokens // phases
-    half = chunk // 2
+    quarter = chunk // 2
+    quarters = 2 * phases
     slots = texts // phases
     loads = [
         pltpu.make_async_copy(src, dst, load_sem.at[i])
@@ -125,7 +129,7 @@
         )
 
     def outward(by, c):
-        rows = pl.ds(c * chunk, chunk)
+        rows = pl.ds(c * quarter, quarter)
         return copy(
             normed.at[rows],
             theirs.at[by - 1, rows],
@@ -135,7 +139,7 @@
         )
 
     def homeward(by, c):
-        rows = pl.ds(c * half, half)
+        rows = pl.ds(c * quarter, quarter)
         return copy(
             theirs.at[by - 1, rows],
             parts.at[by - 1, rows],
@@ -153,20 +157,45 @@
             hidden[rows, :].astype(F32), ln_gain[...], ln_bias[...]
         ).astype(BF16)
 
+    def go_out(c):
+        for by in range(1, n):
+            outward(by, c).start()
+
+    def go_home(c):
+        for by in range(1, n):
+            homeward(by, c).start()
+
     normalise(0)
     pl.semaphore_wait(barrier, n + 2 + window - 1)
-    for c in range(phases):
-        if c > 0:
-            normalise(c)
-        for by in range(1, n):
-            outward(by, c).start()
+    go_out(0)
+    go_out(1)
 
     def teach(s, _):
-        lesson(s, dp).start()
+        turned = teacher[s].astype(F32).T
+        for f in range(n):
+            for h in range(phases):
+                low = (f * phases + h) * slots
+                slabs[s, h, f * slots : (f + 1) * slots, :] = turned[low : low + slots].astype(
+                    BF16
+                )
+
+        @pl.when(s > 0)
+        def _():
+            lesson(s, dp).start()
+
         return 0
 
-    lax.fori_loop(1, window, teach, 0)
+    lax.fori_loop(0, window, teach, 0)
     tiles[dp] = slabs[0]
+    for c in range(1, phases):
+        normalise(c)
+    for f in range(n):
+
+        @pl.when(me == f)
+        def _():
+            bias[...] = fc1_bias[f * units : (f + 1) * units].reshape(1, units)
+
+    kept_rows[...] = (text_ids[...] != 0).astype(F32).T
     picture = unit_rows(images[...].astype(F32)).astype(BF16)
     loads[0].wait()
     loads[1].wait()
@@ -178,21 +207,17 @@
             pre = lax.dot_general(
                 values, fc1[low:high, :], (((1,), (1,)), ((), ())), preferred_element_type=F32
             )
-            bias = fc1_bias[pl.ds(me, 1), low:high]
-            act = jax.nn.gelu(pre + bias, approximate=True).astype(BF16)
+            act = jax.nn.gelu(pre + bias[:, low:high], approximate=True).astype(BF16)
             term = jnp.dot(act, fc2[low:high, :], preferred_element_type=F32)
             mixed = term if mixed is None else mixed + term
         return mixed
 
-    def own_step(c, _):
-        rows = pl.ds(pl.multiple_of(c * chunk, chunk), chunk)
+    def own(c):
+        rows = pl.ds(c * chunk, chunk)
         total[rows, :] = mlp(normed[rows, :]) + hidden[rows, :].astype(F32) + fc2_bias[...]
-        return 0
-
-    lax.fori_loop(0, phases, own_step, 0)
-
-    def their_step(c, _):
-        rows = pl.ds(pl.multiple_of(c * chunk, chunk), chunk)
+
+    def their(c):
+        rows = pl.ds(pl.multiple_of(c * quarter, quarter), quarter)
         for by in range(1, n):
             outward(by, c).wait_recv()
 
@@ -201,17 +226,17 @@
             return 0
 
         lax.fori_loop(0, n - 1, one, 0)
-        for by in range(1, n):
-            homeward(by, 2 * c).start()
-
-        @pl.when(c < phases - 1)
-        def _():
-            for by in range(1, n):
-                homeward(by, 2 * c + 1).start()
-
+
+    def early(c, _):
+        their(c)
+        go_home(c)
+        go_out(c + 2)
         return 0
 
-    lax.fori_loop(0, phases, their_step, 0)
+    own(0)
+    lax.fori_loop(0, 2, early, 0)
+    own(1)
+    their(2)
     loads[2].wait()
 
     def embed(c):
@@ -222,7 +247,7 @@
             homeward(by, 2 * c + 1).wait_recv()
             out = out + parts[by - 1, rows, :].astype(F32)
         final = layer_norm(out, final_gain[...], final_bias[...])
-        kept = (text_ids[pl.ds(c * slots, slots), :] != 0).astype(F32)
+        kept = kept_rows[pl.ds(c * slots, slots), :]
         summed = jnp.sum(final.reshape(slots, seq, width) * kept[:, :, None], axis=1)
         pooled = summed / jnp.sum(kept, axis=1, keepdims=True)
         emb = (
@@ -248,24 +273,30 @@
     to_right = ring // 2
     to_left = ring - 1 - to_right
 
-    def circulate(h):
+    def side_in(h):
         for by in range(1, n):
             block = part(h, lax.rem(me - by + n, n))
             copy(block, block, side_send.at[h, by - 1], side_recv.at[h, by - 1], ahead(by)).wait_recv()
-        twins = 0
-        for step in range(to_right + 1):
+
+    def set_off(h):
+        block = every.at[h, dp]
+        begin(block, right_send.at[h, 0], right_recv.at[h, 0], (right, me))
+        if to_left > 0:
+            begin(block, left_send.at[h, 0], left_recv.at[h, 0], (left, me))
+        begin(block, twin_send.at[h, 0], twin_recv.at[h, 0], (twin, me))
+
+    def circulate(h):
+        twins = 1
+        for step in range(1, to_right + 1):
             block = every.at[h, at_place(place - step, core)]
-            if step > 0:
-                copy(
-                    block, block, right_send.at[h, step - 1], right_recv.at[h, step - 1], (right, me)
-                ).wait_recv()
+            copy(
+                block, block, right_send.at[h, step - 1], right_recv.at[h, step - 1], (right, me)
+            ).wait_recv()
             if step < to_right:
                 begin(block, right_send.at[h, step], right_recv.at[h, step], (right, me))
-            if step == 0 and to_left > 0:
-                begin(block, left_send.at[h, 0], left_recv.at[h, 0], (left, me))
             begin(block, twin_send.at[h, twins], twin_recv.at[h, twins], (twin, me))
             twins += 1
-            if 0 < step <= to_left:
+            if step <= to_left:
                 block = every.at[h, at_place(place + step, core)]
                 copy(
                     block, block, left_send.at[h, step - 1], left_recv.at[h, step - 1], (left, me)
@@ -309,18 +340,20 @@
         lesson(s, later(-s)).wait_recv()
         return 0
 
-    for h in range(phases):
-        exchange(h)
-        if h == 0:
-            for by in range(1, n):
-                homeward(by, 2 * phases - 1).start()
-        circulate(h)
-        if h == 0:
-            lax.fori_loop(1, window, taught, 0)
-            grad[...] = gradient(h)
-        else:
-            grad[...] += gradient(h)
-    grad[...] = scale * grad[...]
+    exchange(0)
+    go_home(2)
+    side_in(0)
+    set_off(0)
+    their(3)
+    go_home(3)
+    circulate(0)
+    lax.fori_loop(1, window, taught, 0)
+    grad[...] = gradient(0)
+    exchange(1)
+    side_in(1)
+    set_off(1)
+    circulate(1)
+    grad[...] += gradient(1)
 
     def told(s, _):
         lesson(s, dp).wait_send()
@@ -328,9 +361,8 @@
 
     lax.fori_loop(1, window, told, 0)
     for by in range(1, n):
-        for c in range(phases):
+        for c in range(quarters):
             outward(by, c).wait_send()
-        for c in range(2 * phases):
             homeward(by, c).wait_send()
     for out in sent:
         out.wait_send()
@@ -355,7 +387,7 @@
     logit_bias,
 ):
     tokens, width = hidden.shape
-    texts, seq = text_ids.shape
+    texts = text_ids.shape[0]
     units = fc1_weight.shape[1]
     group, window, pictures = teacher_logits.shape
     n = lax.axis_size("fsdp")
@@ -364,20 +396,20 @@
     slots = texts // phases
     others = max(n - 1, 1)
 
-    slabs = jnp.transpose(
-        teacher_logits.reshape(n, phases, slots, window, pictures), (3, 1, 0, 2, 4)
-    ).reshape(window, phases, n * slots, pictures)
     vmem = pl.BlockSpec(memory_space=pltpu.VMEM)
     smem = pl.BlockSpec(memory_space=pltpu.SMEM)
     hbm = pl.BlockSpec(memory_space=pl.ANY)
     dma = pltpu.SemaphoreType.DMA
     ring = count // 2
-    return pl.pallas_call(
+    total = pl.pallas_call(
         functools.partial(tower_kernel, n, count, 768),
         out_shape=jax.ShapeDtypeStruct((pictures, width), F32),
         in_specs=[vmem] * 4 + [hbm, vmem, hbm, vmem, vmem, vmem, hbm, vmem, vmem, vmem, smem, smem],
         out_specs=vmem,
         scratch_shapes=[
+            pltpu.VMEM((window, phases, n * slots, pictures), BF16),
+            pltpu.VMEM((1, units), F32),
+            pltpu.VMEM((texts, text_ids.shape[1]), F32),
             pltpu.VMEM((units, width), BF16),
             pltpu.VMEM(fc2_weight.shape, BF16),
             pltpu.VMEM(head_weight.shape, BF16),
@@ -388,8 +420,8 @@
             pltpu.VMEM((phases, count, n * slots, width), BF16),
             pltpu.VMEM((count, phases, n * slots, pictures), BF16),
             dma((3,)),
-            dma((others, phases)),
-            dma((others, phases)),
+            dma((others, 2 * phases)),
+            dma((others, 2 * phases)),
             dma((others, 2 * phases)),
             dma((others, 2 * phases)),
             dma((window,)),
@@ -408,11 +440,11 @@
         ),
     )(
         hidden,
-        text_ids,
+        text_ids.T,
         ln_gain,
         ln_bias,
         fc1_weight.T,
-        fc1_bias.reshape(n, units),
+        fc1_bias,
         fc2_weight,
         fc2_bias,
         final_gain,
@@ -420,10 +452,11 @@
         head_weight,
         head_bias,
         image_emb,
-        slabs,
+        jnp.transpose(teacher_logits, (1, 2, 0)),
         logit_scale,
         logit_bias,
     )
+    return logit_scale[0] * total
 
 
 def solution(mesh):

time: 99 us -> 88.1 us (0.89)
  Pallas kernels: 90.1 us -> 83.5 us
  local copies, waits for them, and re-layouts: 6.08 us -> 0 us
  other arithmetic: 0 us -> 1.58 us
    pallas_call x1, Pallas kernels: 90.1 us -> 83.5 us  [on_device(): pl.pallas_call(functools.partial(tower_kernel, n, count, 768), out_shape=...]
    unnamed x3 -> x0, local copies, waits for them, and re-layouts: 3.98 us -> none
    mul x0 -> x1, other arithmetic: none -> 1.58 us  [on_device(): return logit_scale[0] * total]
    reshape x1 -> x0, local copies, waits for them, and re-layouts: 1.41 us -> none  [on_device(): fc1_bias.reshape(n, units)]
where the time goes in v3:
time: 88.1 us; the launch traced here: 86.4 us
  Pallas kernels  83.5 us (95%)
  other arithmetic  1.58 us (2%)
  between operations  1.31 us (1%)
    pallas_call x1, Pallas kernels, on_device(): pl.pallas_call(functools.partial(tower_kernel, n, count, 768), out_shape=...  83.5 us

profile of v3, /device:TPU:0, one launch (start us, length us, event | category | flops | bytes accessed | tf_op | source)
XLA Modules:
  0.0 86.4 jit_solution(12145774557171540466)
XLA Ops:
  1.3 83.5 %shard_map.154 = f32[32,1152]{1,0:T(8,128)} custom-call(bf16[512,1152]{1,0:T(8,128)(2,1)} %hidden.1, s32[16,32]{1,0:T(8,128)} %bitcast.7, f32[1152]{0:T(1024)} %ln_gain.1, f32[1152]{0:T(1024)} %ln_bias.1, bf16[2152,1152]{1,0:T(8,128)(2,1)} %bitcast.5, f32[4304]{0:T(1024)} %fc1_bias.1, bf16[2152,1152]{1,0:T(8,128)(2,1)} %fc2_hbm.1, f32[1152]{0:T(1024)} %fc2_bias.1, ...), custom_call_target="tpu_custom_call" | custom-call | flops 10154409984 | bytes 9916416 | tf_op jit(solution)/shard_map/pallas_call | solution.py:404
  84.8 1.6 %broadcast_multiply_fusion = f32[32,1152]{1,0:T(8,128)} fusion(f32[32,1152]{1,0:T(8,128)} %shard_map.154, f32[]{:T(128)} %bitcast.4), kind=kLoop, calls=%fused_computation | loop fusion | flops 36864 | bytes 294916 | tf_op jit(solution)/shard_map/mul | solution.py:459

commit v4 on v3

--- a/solution.py
+++ b/solution.py
@@ -78,7 +78,7 @@
     seq, texts = text_ids.shape
     units = fc1.shape[0]
     window = slabs.shape[0]
-    phases, _, rows_here, _ = every.shape
+    phases, _, pairs, rows_here, _ = every.shape
     chunk = tokens // phases
     quarter = chunk // 2
     quarters = 2 * phases
@@ -149,7 +149,7 @@
         )
 
     def lesson(s, block):
-        return copy(slabs.at[s], tiles.at[block], teach_send.at[s], teach_recv.at[s], (later(s), me))
+        return copy(slabs.at[s], tiles.at[lax.rem(block, 2), block // 2], teach_send.at[s], teach_recv.at[s], (later(s), me))
 
     def normalise(c):
         rows = pl.ds(c * chunk, chunk)
@@ -186,7 +186,7 @@
         return 0
 
     lax.fori_loop(0, window, teach, 0)
-    tiles[dp] = slabs[0]
+    tiles[core, dp // 2] = slabs[0]
     for c in range(1, phases):
         normalise(c)
     for f in range(n):
@@ -263,10 +263,10 @@
         sent.append(out)
 
     def part(h, f):
-        return every.at[h, dp, pl.ds(pl.multiple_of(f * slots, slots), slots)]
+        return every.at[h, core, dp // 2, pl.ds(pl.multiple_of(f * slots, slots), slots)]
 
     def exchange(h):
-        every[h, dp, pl.ds(pl.multiple_of(me * slots, slots), slots), :] = embed(h)
+        every[h, core, dp // 2, pl.ds(pl.multiple_of(me * slots, slots), slots), :] = embed(h)
         for by in range(1, n):
             begin(part(h, me), side_send.at[h, by - 1], side_recv.at[h, by - 1], ahead(by))
 
@@ -279,7 +279,7 @@
             copy(block, block, side_send.at[h, by - 1], side_recv.at[h, by - 1], ahead(by)).wait_recv()
 
     def set_off(h):
-        block = every.at[h, dp]
+        block = every.at[h, core, dp // 2]
         begin(block, right_send.at[h, 0], right_recv.at[h, 0], (right, me))
         if to_left > 0:
             begin(block, left_send.at[h, 0], left_recv.at[h, 0], (left, me))
@@ -288,7 +288,7 @@
     def circulate(h):
         twins = 1
         for step in range(1, to_right + 1):
-            block = every.at[h, at_place(place - step, core)]
+            block = every.at[h, core, at_place(place - step, 0) // 2]
             copy(
                 block, block, right_send.at[h, step - 1], right_recv.at[h, step - 1], (right, me)
             ).wait_recv()
@@ -297,7 +297,7 @@
             begin(block, twin_send.at[h, twins], twin_recv.at[h, twins], (twin, me))
             twins += 1
             if step <= to_left:
-                block = every.at[h, at_place(place + step, core)]
+                block = every.at[h, core, at_place(place + step, 0) // 2]
                 copy(
                     block, block, left_send.at[h, step - 1], left_recv.at[h, step - 1], (left, me)
                 ).wait_recv()
@@ -305,13 +305,15 @@
                     begin(block, left_send.at[h, step], left_recv.at[h, step], (left, me))
                 begin(block, twin_send.at[h, twins], twin_recv.at[h, twins], (twin, me))
                 twins += 1
+
+    def twins_in(h):
         twins = 0
         for step in range(to_right + 1):
             sources = [place - step]
             if 0 < step <= to_left:
                 sources.append(place + step)
             for source in sources:
-                block = every.at[h, at_place(source, 1 - core)]
+                block = every.at[h, 1 - core, at_place(source, 0) // 2]
                 copy(
                     block, block, twin_send.at[h, twins], twin_recv.at[h, twins], (twin, me)
                 ).wait_recv()
@@ -320,18 +322,19 @@
     scale = scale_ref[0]
     offset = offset_ref[0]
     pictures = images.shape[0]
-    span = (count, rows_here, pictures)
-    behind = dp - lax.broadcasted_iota(jnp.int32, span, 0)
-    met = jnp.where(behind < 0, behind + count, behind) < window
-
-    def gradient(h):
-        group = every[h].reshape(count * rows_here, width)
+    span = (pairs, rows_here, pictures)
+    pair = lax.broadcasted_iota(jnp.int32, span, 0)
+
+    def gradient(h, side):
+        group = every[h, side].reshape(pairs * rows_here, width)
         dots = lax.dot_general(
             group, picture, (((1,), (1,)), ((), ())), preferred_element_type=F32
         )
         score = (scale * dots + offset).reshape(span)
-        gap = jax.nn.sigmoid(score) - jax.nn.sigmoid(tiles[:, h].astype(F32))
-        weight = jnp.where(met, gap, 0.0).astype(BF16).reshape(count * rows_here, pictures)
+        gap = jax.nn.sigmoid(score) - jax.nn.sigmoid(tiles[side, :, h].astype(F32))
+        behind = dp - side - 2 * pair
+        met = jnp.where(behind < 0, behind + count, behind) < window
+        weight = jnp.where(met, gap, 0.0).astype(BF16).reshape(pairs * rows_here, pictures)
         return lax.dot_general(
             weight, group, (((0,), (0,)), ((), ())), preferred_element_type=F32
         )
@@ -347,13 +350,16 @@
     their(3)
     go_home(3)
     circulate(0)
+    twins_in(0)
     lax.fori_loop(1, window, taught, 0)
-    grad[...] = gradient(0)
     exchange(1)
+    grad[...] = gradient(0, core) + gradient(0, 1 - core)
     side_in(1)
     set_off(1)
     circulate(1)
-    grad[...] += gradient(1)
+    grad[...] += gradient(1, core)
+    twins_in(1)
+    grad[...] += gradient(1, 1 - core)
 
     def told(s, _):
         lesson(s, dp).wait_send()
@@ -417,8 +423,8 @@
             pltpu.VMEM((tokens, width), F32),
             pltpu.VMEM((others, tokens, width), BF16),
             pltpu.VMEM((others, tokens, width), BF16),
-            pltpu.VMEM((phases, count, n * slots, width), BF16),
-            pltpu.VMEM((count, phases, n * slots, pictures), BF16),
+            pltpu.VMEM((phases, 2, count // 2, n * slots, width), BF16),
+            pltpu.VMEM((2, count // 2, phases, n * slots, pictures), BF16),
             dma((3,)),
             dma((others, 2 * phases)),
             dma((others, 2 * phases)),

time: 88.1 us -> 86.7 us (0.984)
  no operation moved by 1% of the time
where the time goes in v4:
time: 86.7 us; the launch traced here: 85.6 us
  Pallas kernels  82.7 us (95%)
  other arithmetic  1.58 us (2%)
  between operations  1.31 us (2%)
    pallas_call x1, Pallas kernels, on_device(): pl.pallas_call(functools.partial(tower_kernel, n, count, 768), out_shape=...  82.7 us

profile of v4, /device:TPU:0, one launch (start us, length us, event | category | flops | bytes accessed | tf_op | source)
XLA Modules:
  0.0 85.6 jit_solution(4487747405578692464)
XLA Ops:
  1.3 82.7 %shard_map.154 = f32[32,1152]{1,0:T(8,128)} custom-call(bf16[512,1152]{1,0:T(8,128)(2,1)} %hidden.1, s32[16,32]{1,0:T(8,128)} %bitcast.7, f32[1152]{0:T(1024)} %ln_gain.1, f32[1152]{0:T(1024)} %ln_bias.1, bf16[2152,1152]{1,0:T(8,128)(2,1)} %bitcast.5, f32[4304]{0:T(1024)} %fc1_bias.1, bf16[2152,1152]{1,0:T(8,128)(2,1)} %fc2_hbm.1, f32[1152]{0:T(1024)} %fc2_bias.1, ...), custom_call_target="tpu_custom_call" | custom-call | flops 10154409984 | bytes 9916416 | tf_op jit(solution)/shard_map/pallas_call | solution.py:410
  84.0 1.6 %broadcast_multiply_fusion = f32[32,1152]{1,0:T(8,128)} fusion(f32[32,1152]{1,0:T(8,128)} %shard_map.154, f32[]{:T(128)} %bitcast.4), kind=kLoop, calls=%fused_computation | loop fusion | flops 36864 | bytes 294916 | tf_op jit(solution)/shard_map/mul | solution.py:465

commit v5 on v4

--- a/solution.py
+++ b/solution.py
@@ -237,6 +237,7 @@
     lax.fori_loop(0, 2, early, 0)
     own(1)
     their(2)
+    go_home(2)
     loads[2].wait()
 
     def embed(c):
@@ -344,7 +345,6 @@
         return 0
 
     exchange(0)
-    go_home(2)
     side_in(0)
     set_off(0)
     their(3)

time: 86.7 us -> 92 us (1.061)
  Pallas kernels: 82.7 us -> 88.7 us
    pallas_call x1, Pallas kernels: 82.7 us -> 88.7 us  [on_device(): pl.pallas_call(functools.partial(tower_kernel, n, count, 768), out_shape=...]
where the time goes in v5:
time: 92 us; the launch traced here: 91.6 us
  Pallas kernels  88.7 us (96%)
  other arithmetic  1.58 us (2%)
  between operations  1.31 us (1%)
    pallas_call x1, Pallas kernels, on_device(): pl.pallas_call(functools.partial(tower_kernel, n, count, 768), out_shape=...  88.7 us

profile of v5, /device:TPU:0, one launch (start us, length us, event | category | flops | bytes accessed | tf_op | source)
XLA Modules:
  0.0 91.6 jit_solution(9975043642556895726)
XLA Ops:
  1.3 88.7 %shard_map.154 = f32[32,1152]{1,0:T(8,128)} custom-call(bf16[512,1152]{1,0:T(8,128)(2,1)} %hidden.1, s32[16,32]{1,0:T(8,128)} %bitcast.7, f32[1152]{0:T(1024)} %ln_gain.1, f32[1152]{0:T(1024)} %ln_bias.1, bf16[2152,1152]{1,0:T(8,128)(2,1)} %bitcast.5, f32[4304]{0:T(1024)} %fc1_bias.1, bf16[2152,1152]{1,0:T(8,128)(2,1)} %fc2_hbm.1, f32[1152]{0:T(1024)} %fc2_bias.1, ...), custom_call_target="tpu_custom_call" | custom-call | flops 10154409984 | bytes 9916416 | tf_op jit(solution)/shard_map/pallas_call | solution.py:410
  90.0 1.6 %broadcast_multiply_fusion = f32[32,1152]{1,0:T(8,128)} fusion(f32[32,1152]{1,0:T(8,128)} %shard_map.154, f32[]{:T(128)} %bitcast.4), kind=kLoop, calls=%fused_computation | loop fusion | flops 36864 | bytes 294916 | tf_op jit(solution)/shard_map/mul | solution.py:465
